TPU v7x, 32 devices: a whole 2x2x4 slice. The times are simulated.
32 devices in a mesh: grp: 2 (over core), dp: 16 (over z, y, x).
Axes of the slice: x: 2, y: 2, z: 4, core: 2. Of those that a mesh axis runs over, the one named last changes fastest.
Arguments:
- question_ids: int32 [512, 64], P(('grp', 'dp')), may hold values from 0 to 30719
- passage_ids: int32 [1024, 256], P(('grp', 'dp')), may hold values from 0 to 30719
- question_lengths: int32 [512], P(('grp', 'dp')), may hold values from 16 to 64
- passage_lengths: int32 [1024], P(('grp', 'dp')), may hold values from 64 to 256
- question_keys: int32 [512], P(('grp', 'dp')), may hold values from 0 to 15
- passage_keys: int32 [1024], P(('grp', 'dp')), may hold values from 0 to 15
- question_valid: int32 [512], P(('grp', 'dp')), may hold values 0 or 1
- word_table: float32 [2, 30720, 128], P('grp', 'dp'), may hold values from -0.3125 to 0.3125
- positions: float32 [2, 2, 256, 128], P('grp'), may hold values from -0.3125 to 0.3125
- attention: float32 [2, 2, 128, 512], P('grp'), may hold values from -0.5 to 0.5
- feedforward: float32 [2, 2, 2, 128, 512], P('grp'), may hold values from -0.5 to 0.5
- vectors: float32 [2, 2, 14, 128], P('grp'), as said below
- word_first: float32 [2, 30720, 128], P('grp', 'dp'), may hold values from -8.940697e-08 to 8.940697e-08
- positions_first: float32 [2, 2, 256, 128], P('grp'), may hold values from -3.33786e-06 to 3.33786e-06
- attention_first: float32 [2, 2, 128, 512], P('grp'), may hold values from -3.33786e-06 to 3.33786e-06
- feedforward_first: float32 [2, 2, 2, 128, 512], P('grp'), may hold values from -3.33786e-06 to 3.33786e-06
- vectors_first: float32 [2, 2, 14, 128], P('grp'), may hold values from -1.335144e-05 to 1.335144e-05
- word_second: float32 [2, 30720, 128], P('grp', 'dp'), may hold values from 1.0240082e-15 to 1.6384131e-14
- positions_second: float32 [2, 2, 256, 128], P('grp'), may hold values from 1.1377869e-14 to 1.820459e-13
- attention_second: float32 [2, 2, 128, 512], P('grp'), may hold values from 1.1377869e-14 to 1.820459e-13
- feedforward_second: float32 [2, 2, 2, 128, 512], P('grp'), may hold values from 1.1377869e-14 to 1.820459e-13
- vectors_second: float32 [2, 2, 14, 128], P('grp'), may hold values from 1.820459e-13 to 2.9127345e-12
- word_anchor: float32 [30720, 128], P('dp'), may hold values from -0.3125 to 0.3125
- positions_anchor: float32 [2, 256, 128], replicated, may hold values from -0.3125 to 0.3125
- attention_anchor: float32 [2, 128, 512], replicated, may hold values from -0.5 to 0.5
- feedforward_anchor: float32 [2, 2, 128, 512], replicated, may hold values from -0.5 to 0.5
- vectors_anchor: float32 [2, 14, 128], replicated, as said below
- word_outer: float32 [30720, 128], P('dp'), may hold values from -0.3125 to 0.3125
- positions_outer: float32 [2, 256, 128], replicated, may hold values from -0.3125 to 0.3125
- attention_outer: float32 [2, 128, 512], replicated, may hold values from -0.3125 to 0.3125
- feedforward_outer: float32 [2, 2, 128, 512], replicated, may hold values from -0.3125 to 0.3125
- vectors_outer: float32 [2, 14, 128], replicated, may hold values from -1.25 to 1.25
Outputs:
- loss_sum: float32 [2], P('grp')
- loss_count: float32 [2], P('grp')
- grad_norm: float32 [2], P('grp')
- word_first_next: float32 [2, 30720, 128], P('grp', 'dp')
- positions_first_next: float32 [2, 2, 256, 128], P('grp')
- attention_first_next: float32 [2, 2, 128, 512], P('grp')
- feedforward_first_next: float32 [2, 2, 2, 128, 512], P('grp')
- vectors_first_next: float32 [2, 2, 14, 128], P('grp')
- word_second_next: float32 [2, 30720, 128], P('grp', 'dp')
- positions_second_next: float32 [2, 2, 256, 128], P('grp')
- attention_second_next: float32 [2, 2, 128, 512], P('grp')
- feedforward_second_next: float32 [2, 2, 2, 128, 512], P('grp')
- vectors_second_next: float32 [2, 2, 14, 128], P('grp')
- word_average: float32 [30720, 128], P('dp')
- positions_average: float32 [2, 256, 128], replicated
- attention_average: float32 [2, 128, 512], replicated
- feedforward_average: float32 [2, 2, 128, 512], replicated
- vectors_average: float32 [2, 14, 128], replicated
- word_outer_next: float32 [30720, 128], P('dp')
- positions_outer_next: float32 [2, 256, 128], replicated
- attention_outer_next: float32 [2, 128, 512], replicated
- feedforward_outer_next: float32 [2, 2, 128, 512], replicated
- vectors_outer_next: float32 [2, 14, 128], replicated
- word_weight_next: float32 [2, 30720, 128], P('grp', 'dp')
- positions_weight_next: float32 [2, 2, 256, 128], P('grp')
- attention_weight_next: float32 [2, 2, 128, 512], P('grp')
- feedforward_weight_next: float32 [2, 2, 2, 128, 512], P('grp')
- vectors_weight_next: float32 [2, 2, 14, 128], P('grp')
Inputs may be any that keep to these rules, and one draw needn't show every extreme that they name: `vectors`: rows 0, 5 and 8 are norm gains near one, the others biases. `vectors_anchor`: rows 0, 5 and 8 are norm gains near one, the others biases.
All inputs are finite; a program needn't handle non-finite values. No bound on the sum of `question_valid` on one device may be relied on, other than what follows from the above.
Results may differ from a plain program's by a relative error of at most 0.018.
The roundings to bfloat16 on the way count: a program that leaves them out, or rounds other values in their place, can miss the bound.
Values may be sent and summed in bfloat16 or wider, within the bound.
A program may use at most 256 MiB of HBM per device.

v0:
```python
import functools
import math

import jax
import jax.numpy as jnp
from jax import lax
from jax.experimental import pallas as pl
from jax.experimental.pallas import tpu as pltpu
from jax.sharding import PartitionSpec as P

HEAD = 64
STEP = 5


NORM_EPS = 1e-05
MASKED = -1000000000.0
BETA_ONE = 0.9
BETA_TWO = 0.999
INNER_RATE = 0.05
WEIGHT_DECAY = 0.01
ADAM_EPS = 1e-08
CLIP_LIMIT = 0.01
OUTER_RATE = 0.7
OUTER_MU = 0.9
CONTRACT_ROWS = (((0,), (0,)), ((), ()))
CONTRACT_LAST = (((1,), (1,)), ((), ()))


def layer_norm(values, gain, shift):
    center = values - jnp.mean(values, -1, keepdims=True)
    spread = jnp.mean(center * center, -1, keepdims=True)
    return center * lax.rsqrt(spread + NORM_EPS) * gain + shift


def gelu_tanh(values):
    return jax.nn.gelu(values, approximate=True)


def low16(values):
    return values.astype(jnp.bfloat16)


NEG = -1e30
MESH = pl.DeviceIdType.MESH
VMEM_LIMIT = 60 * 1024 * 1024
WAYS = 4
SLOTS = 128
SPAN = WAYS * SLOTS
CHUNK = 256
UNROLL = 4
RAW_Q = 64
RAW_FLAGS = 72
RAW_ROWS = 80


def greet_all(many):
    me = lax.axis_index("dp")
    barrier = pltpu.get_barrier_semaphore()

    def greet(step, carry):
        peer = lax.rem(me + step, many)
        pl.semaphore_signal(barrier, inc=1, device_id={"dp": peer}, device_id_type=MESH)
        return carry

    lax.fori_loop(1, many, greet, 0)
    return me


def enter(many):
    me = greet_all(many)
    pl.semaphore_wait(pltpu.get_barrier_semaphore(), many - 1)
    return me


def copy_to(peer, src, dst, send, recv):
    return pltpu.make_async_remote_copy(
        src_ref=src,
        dst_ref=dst,
        send_sem=send,
        recv_sem=recv,
        device_id={"dp": peer},
        device_id_type=MESH,
    )


def spread_start(many, me, pairs, send, recv, slot):
    def step_start(step, carry):
        peer = lax.rem(me + step, many)
        for index, (source, landing) in enumerate(pairs):
            copy_to(
                peer,
                source(peer),
                landing.at[me],
                send.at[slot + index, peer],
                recv.at[slot + index, me],
            ).start()
        return carry

    lax.fori_loop(1, many, step_start, 0)


def spread_wait(many, me, pairs, send, recv, slot):
    def step_wait(step, carry):
        peer = lax.rem(me + step, many)
        for index, (source, landing) in enumerate(pairs):
            copy = copy_to(
                peer,
                source(peer),
                landing.at[peer],
                send.at[slot + index, peer],
                recv.at[slot + index, peer],
            )
            copy.wait_recv()
            copy.wait_send()
        return carry

    lax.fori_loop(1, many, step_wait, 0)


def dot(left, right):
    return jnp.dot(left, right, preferred_element_type=jnp.float32)


def dot_rows(left, right):
    return lax.dot_general(left, right, CONTRACT_ROWS, preferred_element_type=jnp.float32)


def dot_last(left, right):
    return lax.dot_general(left, right, CONTRACT_LAST, preferred_element_type=jnp.float32)


def iota(shape, axis):
    return lax.broadcasted_iota(jnp.int32, shape, axis)


def hot(mask):
    return jnp.where(mask, 1.0, 0.0).astype(jnp.bfloat16)


def first_kernel(
    sizes,
    question_ref,
    passage_ref,
    length_q,
    length_p,
    key_q,
    valid_q,
    key_p,
    table_ref,
    place_ref,
    every_ref,
    rows_ref,
    kept_ref,
    entry_ref,
    count_ref,
    stage,
    raw,
    ask,
    asks,
    low_ref,
    offer,
    landed,
    own,
    table_t,
    place_t,
    send,
    recv,
):
    many = sizes.many
    count_q, count_p = sizes.count
    each = count_q + count_p
    depth = sizes.depth
    half = count_q // 2
    me = greet_all(many)
    lane = iota((1, 128), 1)
    for seq in range(count_p):
        stop = length_p[seq]
        stage[seq : seq + 1, :] = jnp.where(lane < stop, passage_ref[seq : seq + 1, 0:128], -1)
        stage[count_p + seq : count_p + seq + 1, :] = jnp.where(
            lane + 128 < stop, passage_ref[seq : seq + 1, 128:256], -1
        )
    both = jnp.concatenate([question_ref[0:half, :], question_ref[half:count_q, :]], 1)
    for seq in range(half):
        stop = jnp.where(lane < 64, length_q[seq], length_q[half + seq] + 64)
        stage[RAW_Q + seq : RAW_Q + seq + 1, :] = jnp.where(lane < stop, both[seq : seq + 1], -1)
    flags = jnp.zeros((1, 128), jnp.int32)
    for spot in range(count_q):
        flags = jnp.where(lane == spot, key_q[spot], flags)
        flags = jnp.where(lane == count_q + spot, valid_q[spot], flags)
    for spot in range(count_p):
        flags = jnp.where(lane == 2 * count_q + spot, key_p[spot], flags)
    stage[RAW_FLAGS:RAW_ROWS, :] = jnp.broadcast_to(flags, (8, 128))
    raw[...] = stage[...].astype(jnp.int16)
    heads = jnp.concatenate([question_ref[:, 0:1], passage_ref[:, 0:1]], 0)
    diagonal = iota((each, 128), 0) == iota((each, 128), 1)
    heads = jnp.sum(jnp.where(diagonal, jnp.broadcast_to(heads, (each, 128)), 0), 0, keepdims=True)
    ask[...] = jnp.broadcast_to(heads, (8, 128))
    pl.semaphore_wait(pltpu.get_barrier_semaphore(), many - 1)
    ask_pairs = [(lambda peer: ask, asks)]
    raw_pairs = [(lambda peer: raw, every_ref)]
    spread_start(many, me, ask_pairs, send, recv, 0)
    spread_start(many, me, raw_pairs, send, recv, 1)
    asks[me] = ask[...]
    every_ref[me] = raw[...]
    padded = sizes.padded
    if padded > depth:
        low_ref[...] = jnp.zeros_like(low_ref)
    low_ref[0:depth, :] = low16(table_ref[...])
    first = me * depth
    block = math.gcd(many, 16)
    spread_wait(many, me, ask_pairs, send, recv, 0)

    def pick(step, carry):
        found = []
        for i in range(block):
            line = jnp.broadcast_to(asks[step * block + i][0:1, :].astype(jnp.float32), (each, 128))
            found.append(jnp.sum(jnp.where(diagonal, line, 0.0), 1, keepdims=True))
        place = jnp.concatenate(found, 0).astype(jnp.int32) - first
        spot = jnp.where((place >= 0) & (place < depth), place, -1)
        number = spot.shape[0]
        total = jnp.zeros((number, 128), jnp.float32)
        wide = jnp.broadcast_to(spot, (number, CHUNK))
        for at in range(padded // CHUNK):
            chosen = hot(wide == iota((number, CHUNK), 1) + at * CHUNK)
            total += dot(chosen, low_ref[at * CHUNK : (at + 1) * CHUNK, :])
        for i in range(block):
            offer[step * block + i] = low16(total[i * each : (i + 1) * each])
        return carry

    lax.fori_loop(0, many // block, pick, 0)
    offer_pairs = [(lambda peer: offer.at[peer], landed)]
    spread_start(many, me, offer_pairs, send, recv, 2)
    landed[me] = offer[me]
    if sizes.keep:
        prepare_tokens(sizes, table_ref, place_ref, table_t, place_t)
    spread_wait(many, me, raw_pairs, send, recv, 1)

    def spans_of(enc, count):
        def spans(turn, count):
            steps = [turn * sizes.unroll[enc] + u for u in range(sizes.unroll[enc])]
            packed = [pack_span(sizes, enc, s, 0, first, every_ref) for s in steps]
            found = [gather_span(sizes, enc, part[0], table_t, place_t) for part in packed]
            for part in packed:
                count = jnp.maximum(count, part[1])
            for u, s in enumerate(steps):
                at = s if enc == 0 else sizes.steps[0] + s
                kept_ref[at, 0:128, :] = found[u][0]
                kept_ref[at, 128:129, :] = found[u][1]
                entry_ref[at, 0:1, :] = packed[u][0]
            return count

        return lax.fori_loop(0, sizes.steps[enc] // sizes.unroll[enc], spans, count)

    count = jnp.zeros((8, 128), jnp.float32)
    if sizes.keep:
        count = spans_of(0, count)
    spread_wait(many, me, offer_pairs, send, recv, 2)
    own[...] = low16(jnp.sum(landed[...].astype(jnp.float32), 0))
    row_pairs = [(lambda peer: own, rows_ref)]
    spread_start(many, me, row_pairs, send, recv, 3)
    rows_ref[me] = own[...]
    if sizes.keep:
        count = spans_of(1, count)
    count_ref[...] = count
    spread_wait(many, me, row_pairs, send, recv, 3)


def first_stage(sizes, ids_q, ids_p, length_q, length_p, key_q, valid_q, key_p, table, positions):
    many = sizes.many
    padded = sizes.padded
    both = sum(sizes.count)
    vm = pl.BlockSpec(memory_space=pltpu.VMEM)
    sm = pl.BlockSpec(memory_space=pltpu.SMEM)
    kept = sizes.spans if sizes.keep else 1
    return pl.pallas_call(
        functools.partial(first_kernel, sizes),
        out_shape=(
            jax.ShapeDtypeStruct((many, RAW_ROWS, 128), jnp.int16),
            jax.ShapeDtypeStruct((many, both, 128), jnp.bfloat16),
            jax.ShapeDtypeStruct((kept, 136, SPAN), jnp.float32),
            jax.ShapeDtypeStruct((kept, 8, SPAN), jnp.int32),
            jax.ShapeDtypeStruct((8, 128), jnp.float32),
        ),
        in_specs=[vm, vm, sm, sm, sm, sm, sm, vm, vm],
        out_specs=[vm] * 5,
        scratch_shapes=[
            pltpu.VMEM((RAW_ROWS, 128), jnp.int32),
            pltpu.VMEM((RAW_ROWS, 128), jnp.int16),
            pltpu.VMEM((8, 128), jnp.int32),
            pltpu.VMEM((many, 8, 128), jnp.int32),
            pltpu.VMEM((padded, 128), jnp.bfloat16),
            pltpu.VMEM((many, both, 128), jnp.bfloat16),
            pltpu.VMEM((many, both, 128), jnp.bfloat16),
            pltpu.VMEM((both, 128), jnp.bfloat16),
            pltpu.VMEM((128, padded), jnp.bfloat16),
            pltpu.VMEM((2, 2, 128, CHUNK), jnp.bfloat16),
            pltpu.SemaphoreType.DMA((4, many)),
            pltpu.SemaphoreType.DMA((4, many)),
        ],
        compiler_params=pltpu.CompilerParams(
            collective_id=1, has_side_effects=True, vmem_limit_bytes=VMEM_LIMIT
        ),
        name="first_stage",
    )(ids_q, ids_p, length_q, length_p, key_q, valid_q, key_p, table, positions)


def norm_rows(values, gain, shift):
    center = values - jnp.mean(values, -1, keepdims=True)
    spread = jnp.mean(center * center, -1, keepdims=True)
    return center * lax.rsqrt(spread + NORM_EPS) * gain + shift


def two_heads(values):
    lane = iota(values.shape, 1)
    low = jnp.where(lane < HEAD, values, jnp.zeros_like(values))
    high = jnp.where(lane >= HEAD, values, jnp.zeros_like(values))
    return jnp.concatenate([low, high], 0)


def merge_heads(both):
    half = both.shape[0] // 2
    lane = iota((half, both.shape[1]), 1)
    return jnp.where(lane < HEAD, both[:half], both[half:])


class Sizes:
    def __init__(self, many, count_q, count_p, depth):
        self.many = many
        self.count = (count_q, count_p)
        self.depth = depth
        self.padded = -(-depth // CHUNK) * CHUNK
        self.steps = (many // (2 * WAYS), many)
        self.unroll = tuple(math.gcd(UNROLL, step) for step in self.steps)
        self.spans = self.steps[0] + self.steps[1]
        self.devices = (2 * WAYS, 1)
        self.queries = (2 * WAYS * count_q, count_p)
        self.lines = 1024 // many
        self.kind = jnp.bfloat16 if self.lines % 16 == 0 else jnp.float32
        self.keep = self.spans * 136 * SPAN * 4 <= 8 * 1024 * 1024


def vector_row(vec_ref, enc, row):
    return vec_ref[0, row, enc : enc + 1, :]


def prepare_tokens(sizes, table_ref, place_ref, table_t, place_t):
    depth = sizes.depth
    if sizes.padded > depth:
        table_t[...] = jnp.zeros_like(table_t)

    def turn(step, carry):
        spot = pl.ds(pl.multiple_of(step * 128, 128), 128)
        table_t[:, spot] = low16(jnp.transpose(table_ref[spot, :]))
        return carry

    whole = depth // 128
    lax.fori_loop(0, whole, turn, 0)
    rest = depth - whole * 128
    if rest:
        piece = jnp.concatenate([table_ref[whole * 128 :, :], jnp.zeros((128 - rest, 128), jnp.float32)], 0)
        table_t[:, whole * 128 : (whole + 1) * 128] = low16(jnp.transpose(piece))

    def turn_place(step, carry):
        enc, cut = (step // 2, step % 2)
        spot = pl.ds(pl.multiple_of(cut * 128, 128), 128)
        turned = jnp.transpose(place_ref[0, enc, spot, :])
        high = low16(turned)
        place_t[enc, 0, :, spot] = high
        place_t[enc, 1, :, spot] = low16(turned - high.astype(jnp.float32))
        return carry

    lax.fori_loop(0, 4, turn_place, 0)


def prepare_weights(attn_ref, vec_ref, w_kv, vec_t):
    for enc in range(2):
        for cut in range(2):
            w_kv[enc, cut * 128 : (cut + 1) * 128, :] = low16(
                jnp.transpose(attn_ref[0, enc, :, (cut + 1) * 128 : (cut + 2) * 128])
            )
        rows = [vector_row(vec_ref, enc, row) for row in range(4)]
        rows = jnp.concatenate(rows + [jnp.zeros((124, 128), jnp.float32)], 0)
        vec_t[enc] = jnp.transpose(rows)


def lane_pick(values, lanes):
    return jnp.take_along_axis(values, lanes, axis=1, mode="promise_in_bounds")


def pack_span(sizes, enc, step, level, first, raw_ref):
    if enc == 1:
        ids = raw_ref[step, 0:RAW_Q, :].astype(jnp.int32)
    else:
        ids = jnp.concatenate(
            [
                raw_ref[step * 8 + i, RAW_Q:RAW_ROWS, :].astype(jnp.int32)[0:8]
                for i in range(8)
            ],
            0,
        )
    place = ids - first
    owned = (place >= 0) & (place < sizes.depth)
    flag = hot(owned)
    inside = dot(flag, hot(iota((128, 128), 0) <= iota((128, 128), 1))).astype(jnp.int32)
    total = dot(flag, jnp.ones((128, 128), jnp.bfloat16))
    before = dot(hot(iota((64, 64), 1) < iota((64, 64), 0)), low16(total))
    start = before.astype(jnp.int32)
    stop = (before + total).astype(jnp.int32)
    line = iota((64, 128), 0)
    turn = iota((64, 128), 1)
    lane = jnp.zeros((64, 128), jnp.int32)
    for jump in (64, 32, 16, 8, 4, 2, 1):
        seen = lane_pick(inside, lane + (jump - 1))
        lane = jnp.where(seen <= turn, lane + jump, lane)
    row = lane_pick(place, lane)
    if enc == 1:
        where = (line >> 5) * 128 + lane
        seq = (line & 31) + 1
    else:
        where = lane & 63
        seq = (line >> 3) * sizes.count[0] + (lane >> 6) * 8 + (line & 7) + 1
    code = lane_pick((row << 16) + (where << 8) + seq, (turn - start) & 127)
    codes = []
    for window in range(WAYS):
        slot = turn + (window * SLOTS + level * SPAN)
        kept = jnp.where((slot >= start) & (slot < stop), code, 0)
        codes.append(jnp.sum(kept, 0, keepdims=True))
    return jnp.concatenate(codes, 1), (before + total)[56:64]


def gather_span(sizes, enc, code, table_t, place_t, short=False):
    rows = code >> 16
    where = (code >> 8) & 255
    x = jnp.zeros((128, SPAN), jnp.float32)
    wide = jnp.broadcast_to(rows, (CHUNK, SPAN))

    def add(cut, x):
        spot = pl.ds(pl.multiple_of(cut * CHUNK, CHUNK), CHUNK)
        return x + dot(table_t[:, spot], hot(wide == iota((CHUNK, SPAN), 0) + cut * CHUNK))

    x = lax.fori_loop(0, sizes.padded // CHUNK, add, x, unroll=not short)
    chosen = hot(jnp.broadcast_to(where, (CHUNK, SPAN)) == iota((CHUNK, SPAN), 0))
    x += dot(place_t[enc, 0], chosen) + dot(place_t[enc, 1], chosen)
    center = x - jnp.mean(x, 0, keepdims=True)
    rate = lax.rsqrt(jnp.mean(center * center, 0, keepdims=True) + NORM_EPS)
    return center * rate, rate


def project(enc, scaled, vec_t, w_kv):
    a_t = low16(scaled * vec_t[enc, :, 0:1] + vec_t[enc, :, 1:2])
    kv = dot(w_kv[enc], a_t)
    keys_t = low16(kv[:128])
    values_t = low16(kv[128:] + vec_t[enc, :, 3:4])
    return a_t, keys_t, values_t


def own_slots(code, number):
    line = iota((2 * number, SPAN), 0)
    line = jnp.where(line >= number, line - number, line)
    return line == (code & 255) - 1


def forward_kernel(
    sizes,
    raw_ref,
    rows_ref,
    kept_hbm,
    entry_hbm,
    count_ref,
    table_ref,
    place_ref,
    attn_ref,
    vec_ref,
    out_ref,
    lse_ref,
    query_ref,
    levels_ref,
    table_t,
    place_t,
    w_kv,
    vec_t,
    query_q,
    total_q,
    top_q,
    mass_q,
    total_p,
    top_p,
    mass_p,
    kept_ref,
    entry_ref,
    load,
):
    loads = load_kept(sizes, kept_hbm, entry_hbm, kept_ref, entry_ref, load)
    first = lax.axis_index("dp") * sizes.depth
    count_q, count_p = sizes.count
    prepare_weights(attn_ref, vec_ref, w_kv, vec_t)
    begin = 1 if sizes.keep else 0
    count = count_ref[...]
    block = math.gcd(sizes.many, 16)
    for enc in range(2):
        low, high = (0, count_q) if enc == 0 else (count_q, count_q + count_p)
        w_q = low16(attn_ref[0, enc, :, 0:128])

        def ask(step, carry):
            spot = pl.ds(step * block, block)
            held = rows_ref[spot, low:high, :].reshape(block * (high - low), 128)
            x = held.astype(jnp.float32) + place_ref[0, enc, 0:1, :]
            h = norm_rows(x, vector_row(vec_ref, enc, 0), vector_row(vec_ref, enc, 1))
            query = low16(dot(low16(h), w_q) + vector_row(vec_ref, enc, 2))
            query_ref[spot, low:high, :] = query.reshape(block, high - low, 128)
            if enc == 0:
                for half in range(block // 8):
                    query_q[step * (block // 8) + half] = query[half * 8 * count_q : (half + 1) * 8 * count_q]
            return carry

        lax.fori_loop(0, sizes.many // block, ask, 0)
    states = ((total_q, top_q, mass_q), (total_p, top_p, mass_p))
    lse_ref[...] = jnp.full_like(lse_ref, NEG)

    def close(enc, step, total, top, mass):
        some = mass > 0.0
        safe = jnp.where(some, mass, 1.0)
        mixed = merge_heads(total / safe)
        lse = jnp.where(some, top + jnp.log(safe), NEG)
        if enc == 1:
            out_ref[step, count_q:, :] = low16(mixed)
            at = iota(lse.shape, 0) == iota(lse.shape, 1)
            lse_ref[step, 0:1, :] = jnp.sum(jnp.where(at, lse, 0.0), 0, keepdims=True)
        else:
            half = lse.shape[0] // 2
            row = iota((count_q, 128), 0)
            lane = iota((count_q, 128), 1)
            for i in range(8):
                spot = slice(i * count_q, (i + 1) * count_q)
                out_ref[step * 8 + i, 0:count_q, :] = low16(mixed[spot])
                line = jnp.where(lane == row, lse[spot], 0.0) + jnp.where(
                    lane == row + count_q, lse[half + i * count_q : half + (i + 1) * count_q], 0.0
                )
                lse_ref[step * 8 + i, 1:2, :] = jnp.sum(line, 0, keepdims=True)

    def attend(enc, steps, codes, scaleds, olds):
        queries = [query_q[s] if enc == 0 else query_ref[s, count_q:, :] for s in steps]
        made = [project(enc, scaled, vec_t, w_kv) for scaled in scaleds]
        scores = [dot(two_heads(query), part[1]) * HEAD ** (-0.5) for query, part in zip(queries, made)]
        news = []
        for u, score in enumerate(scores):
            mine = own_slots(codes[u], queries[u].shape[0])
            score = jnp.where(mine, score, NEG)
            new = jnp.max(score, 1, keepdims=True)
            if olds is not None:
                new = jnp.maximum(olds[u][1][:, 0:1], new)
            expo = jnp.where(mine, jnp.exp(score - new), 0.0)
            total = dot_last(low16(expo), made[u][2])
            mass = jnp.sum(expo, 1, keepdims=True)
            if olds is not None:
                fade = jnp.exp(olds[u][1] - new)
                total = olds[u][0] * fade + total
                mass = olds[u][2] * fade + mass
            wide = (score.shape[0], 128)
            news.append((total, jnp.broadcast_to(new, wide), jnp.broadcast_to(mass, wide)))
        for u, s in enumerate(steps):
            for ref, value in zip(states[enc], news[u]):
                ref[s] = value
        return news

    for enc in range(2):
        if sizes.keep:
            for copy in loads[2 * enc : 2 * enc + 2]:
                copy.wait()

            def kept_spans(turn, carry):
                steps = [turn * sizes.unroll[enc] + u for u in range(sizes.unroll[enc])]
                ats = [s if enc == 0 else sizes.steps[0] + s for s in steps]
                news = attend(
                    enc, steps, [entry_ref[at, 0:1, :] for at in ats], [kept_ref[at, 0:128, :] for at in ats], None
                )
                for s, new in zip(steps, news):
                    close(enc, s, *new)
                return carry

            lax.fori_loop(0, sizes.steps[enc] // sizes.unroll[enc], kept_spans, 0)
        else:
            total, top, mass = states[enc]
            total[...] = jnp.zeros_like(total)
            mass[...] = jnp.zeros_like(mass)
            top[...] = jnp.full_like(top, NEG)

    def needed(count):
        return jnp.maximum((jnp.max(count).astype(jnp.int32) + SPAN - 1) // SPAN, 1)

    start = needed(count)
    levels_ref[0] = start

    @pl.when(start > begin)
    def _():
        prepare_tokens(sizes, table_ref, place_ref, table_t, place_t)

        def one_level(state):
            level, unused, count = state
            for enc in range(2):

                def one_span(step, count):
                    code, found = pack_span(sizes, enc, step, level, first, raw_ref)
                    scaled = gather_span(sizes, enc, code, table_t, place_t, True)[0]
                    attend(enc, [step], [code], [scaled], [tuple(ref[step] for ref in states[enc])])
                    return jnp.maximum(count, found)

                count = lax.fori_loop(0, sizes.steps[enc], one_span, count)
            return level + 1, needed(count), count

        if sizes.keep:
            lax.fori_loop(
                begin, start, lambda level, carry: one_level((level, carry, count))[1], jnp.int32(0)
            )
        else:
            last = lax.while_loop(
                lambda state: state[0] < state[1], one_level, (jnp.int32(begin), start, count)
            )
            levels_ref[0] = last[1]
        for enc in range(2):

            def close_span(step, carry):
                close(enc, step, *(ref[step] for ref in states[enc]))
                return carry

            lax.fori_loop(0, sizes.steps[enc], close_span, 0)


def load_kept(sizes, kept_hbm, entry_hbm, kept_ref, entry_ref, load):
    if not sizes.keep:
        return []
    copies = []
    for enc, rows in enumerate((slice(0, sizes.steps[0]), slice(sizes.steps[0], sizes.spans))):
        for j, (source, target) in enumerate(((kept_hbm, kept_ref), (entry_hbm, entry_ref))):
            copy = pltpu.make_async_copy(source.at[rows], target.at[rows], load.at[enc, j])
            copy.start()
            copies.append(copy)
    return copies


def kept_scratch(sizes):
    kept = sizes.spans if sizes.keep else 1
    return [
        pltpu.VMEM((kept, 136, SPAN), jnp.float32),
        pltpu.VMEM((kept, 8, SPAN), jnp.int32),
        pltpu.SemaphoreType.DMA((2, 2)),
    ]


def token_scratch(sizes):
    return [
        pltpu.VMEM((128, sizes.padded), jnp.bfloat16),
        pltpu.VMEM((2, 2, 128, CHUNK), jnp.bfloat16),
        pltpu.VMEM((2, 256, 128), jnp.bfloat16),
        pltpu.VMEM((2, 128, 128), jnp.float32),
    ]


def local_call(kernel, out_shape, inputs, scratch, name, smem_in=(), smem_out=(), any_in=()):
    vm = pl.BlockSpec(memory_space=pltpu.VMEM)
    sm = pl.BlockSpec(memory_space=pltpu.SMEM)
    hbm = pl.BlockSpec(memory_space=pl.ANY)
    return pl.pallas_call(
        kernel,
        out_shape=out_shape,
        in_specs=[sm if i in smem_in else hbm if i in any_in else vm for i in range(len(inputs))],
        out_specs=[sm if i in smem_out else vm for i in range(len(out_shape))],
        scratch_shapes=scratch,
        compiler_params=pltpu.CompilerParams(vmem_limit_bytes=VMEM_LIMIT),
        name=name,
    )(*inputs)


def tokens_forward(sizes, every, rows, kept, entry, counted, table, positions, attention, vectors):
    many = sizes.many
    both = sum(sizes.count)
    state = []
    for enc in range(2):
        tall = 2 * sizes.queries[enc]
        state += [pltpu.VMEM((sizes.steps[enc], tall, 128), jnp.float32)] * 3
    return local_call(
        functools.partial(forward_kernel, sizes),
        (
            jax.ShapeDtypeStruct((many, both, 128), jnp.bfloat16),
            jax.ShapeDtypeStruct((many, 2, 128), jnp.float32),
            jax.ShapeDtypeStruct((many, both, 128), jnp.bfloat16),
            jax.ShapeDtypeStruct((1,), jnp.int32),
        ),
        (every, rows, kept, entry, counted, table, positions, attention, vectors),
        token_scratch(sizes)
        + [pltpu.VMEM((sizes.steps[0], sizes.queries[0], 128), jnp.bfloat16)]
        + state
        + kept_scratch(sizes),
        "tokens_forward",
        smem_out=(3,),
        any_in=(2, 3),
    )


def mix_kernel(
    many, count_q, part_ref, lse_ref, mixed_ref, total_ref, landed, landed_lse, own, own_lse, send, recv
):
    me = enter(many)
    pairs = [
        (lambda peer: part_ref.at[peer], landed),
        (lambda peer: lse_ref.at[peer], landed_lse),
    ]
    spread_start(many, me, pairs, send, recv, 0)
    landed[me] = part_ref[me]
    landed_lse[me] = lse_ref[me]
    spread_wait(many, me, pairs, send, recv, 0)
    parts = landed_lse[...]
    top = jnp.max(parts, 0)
    total = top + jnp.log(jnp.sum(jnp.exp(parts - top[None]), 0))
    own_lse[...] = total
    share = jnp.exp(parts - total[None])
    count_p = part_ref.shape[1] - count_q
    mixed = jnp.zeros((count_q + count_p, 128), jnp.float32)
    for peer in range(many):
        factors = []
        for row, number in ((1, count_q), (0, count_p)):
            wide = (2 * number, 128)
            at = iota(wide, 0) == iota(wide, 1)
            line = jnp.broadcast_to(share[peer][row : row + 1], wide)
            column = jnp.sum(jnp.where(at, line, 0.0), 1, keepdims=True)
            lane = iota((number, 128), 1)
            factors.append(jnp.where(lane < HEAD, column[0:number], column[number:]))
        mixed += jnp.concatenate(factors, 0) * landed[peer].astype(jnp.float32)
    own[...] = low16(mixed)
    pairs = [(lambda peer: own, mixed_ref), (lambda peer: own_lse, total_ref)]
    spread_start(many, me, pairs, send, recv, 2)
    mixed_ref[me] = own[...]
    total_ref[me] = own_lse[...]
    spread_wait(many, me, pairs, send, recv, 2)


def remote_call(kernel, out_shape, inputs, scratch, lanes, many, ident, name):
    return pl.pallas_call(
        kernel,
        out_shape=out_shape,
        in_specs=[pl.BlockSpec(memory_space=pltpu.VMEM)] * len(inputs),
        out_specs=[pl.BlockSpec(memory_space=pltpu.VMEM)] * len(out_shape),
        scratch_shapes=scratch
        + [pltpu.SemaphoreType.DMA((lanes, many)), pltpu.SemaphoreType.DMA((lanes, many))],
        compiler_params=pltpu.CompilerParams(
            collective_id=ident, has_side_effects=True, vmem_limit_bytes=VMEM_LIMIT
        ),
        name=name,
    )(*inputs)


def exchange_mixed(sizes, part, lse):
    many = sizes.many
    both = sum(sizes.count)
    return remote_call(
        functools.partial(mix_kernel, many, sizes.count[0]),
        (
            jax.ShapeDtypeStruct((many, both, 128), jnp.bfloat16),
            jax.ShapeDtypeStruct((many, 2, 128), jnp.float32),
        ),
        (part, lse),
        [
            pltpu.VMEM((many, both, 128), jnp.bfloat16),
            pltpu.VMEM((many, 2, 128), jnp.float32),
            pltpu.VMEM((both, 128), jnp.bfloat16),
            pltpu.VMEM((2, 128), jnp.float32),
        ],
        4,
        many,
        2,
        "exchange_mixed",
    )


def backward_kernel(
    sizes,
    levels_ref,
    raw_ref,
    query_ref,
    mixed_ref,
    lse_ref,
    grad_ref,
    kept_hbm,
    entry_hbm,
    table_ref,
    place_ref,
    attn_ref,
    vec_ref,
    d_query_ref,
    d_table_ref,
    slice_ref,
    table_t,
    place_t,
    w_kv,
    vec_t,
    d_place_ref,
    d_attn_ref,
    acc_gain,
    acc_shift,
    acc_value,
    d_query_q,
    d_query_p,
    kept_ref,
    entry_ref,
    load,
):
    loads = load_kept(sizes, kept_hbm, entry_hbm, kept_ref, entry_ref, load)
    first = lax.axis_index("dp") * sizes.depth
    count_q, count_p = sizes.count
    prepare_weights(attn_ref, vec_ref, w_kv, vec_t)
    begin = 1 if sizes.keep else 0
    again = levels_ref[0] > begin

    @pl.when(again)
    def _():
        prepare_tokens(sizes, table_ref, place_ref, table_t, place_t)

    for ref in (d_table_ref, d_place_ref, d_attn_ref, d_query_q, d_query_p, acc_gain, acc_shift, acc_value):
        ref[...] = jnp.zeros_like(ref)

    def ask_span(enc, step):
        if enc == 0:
            spot = pl.ds(step * 8, 8)
            shape = (8 * count_q, 128)
            found = [ref[spot, 0:count_q, :].reshape(shape) for ref in (query_ref, grad_ref, mixed_ref)]
            lines = [jnp.broadcast_to(lse_ref[step * 8 + i, 1:2, :], (count_q, 128)) for i in range(8)]
            lines = jnp.concatenate(lines, 0)
            row = iota(lines.shape, 0) % count_q
            lane = iota(lines.shape, 1)
            lse = [
                jnp.sum(jnp.where(lane == row + head * count_q, lines, 0.0), 1, keepdims=True)
                for head in range(2)
            ]
            lse = jnp.concatenate(lse, 0)
        else:
            found = [ref[step, count_q:, :] for ref in (query_ref, grad_ref, mixed_ref)]
            lines = jnp.broadcast_to(lse_ref[step, 0:1, :], (2 * count_p, 128))
            lse = jnp.sum(jnp.where(iota(lines.shape, 1) == iota(lines.shape, 0), lines, 0.0), 1, keepdims=True)
        return found + [lse]

    def work(enc, steps, codes, scaleds, rates, short=False):
        w_all = low16(attn_ref[0, enc, :, 128:384])
        asked = [ask_span(enc, step) for step in steps]
        made = [project(enc, scaled, vec_t, w_kv) for scaled in scaleds]
        d_queries, d_kvs = ([], [])
        for (query, grad, mixed, lse), code, (a_t, keys_t, values_t) in zip(asked, codes, made):
            both = two_heads(query)
            grads = two_heads(grad)
            base = jnp.sum(
                grads.astype(jnp.float32) * jnp.concatenate([mixed, mixed], 0).astype(jnp.float32),
                1,
                keepdims=True,
            )
            scores = dot(both, keys_t) * HEAD ** (-0.5)
            mine = own_slots(code, query.shape[0])
            probs = jnp.where(mine, jnp.exp(jnp.where(mine, scores, NEG) - lse), 0.0)
            d_probs = dot(grads, values_t)
            d_scores = low16(probs * (d_probs - base))
            d_values = low16(dot_rows(grads, low16(probs)))
            d_keys = low16(dot_rows(both, d_scores) * HEAD ** (-0.5))
            d_queries.append(merge_heads(dot_last(d_scores, keys_t)) * HEAD ** (-0.5))
            d_kvs.append(jnp.concatenate([d_keys, d_values], 0))
        for step, d_query in zip(steps, d_queries):
            if enc == 0:
                d_query_q[step] += d_query
            else:
                d_query_p[step] += d_query
        d_kv = jnp.concatenate(d_kvs, 1)
        a_t = jnp.concatenate([part[0] for part in made], 1)
        scaled = jnp.concatenate(scaleds, 1)
        rate = jnp.concatenate(rates, 1)
        code = jnp.concatenate(codes, 1)
        width = code.shape[1]
        d_attn_ref[enc] += dot_last(a_t, d_kv)
        d_h = dot(w_all, d_kv)
        fold = lambda values: sum(values[:, i * SPAN : (i + 1) * SPAN] for i in range(width // SPAN))
        acc_value[enc] += fold(d_kv[128:].astype(jnp.float32))
        acc_gain[enc] += fold(d_h * scaled)
        acc_shift[enc] += fold(d_h)
        d_scaled = d_h * vec_t[enc, :, 0:1]
        center = d_scaled - jnp.mean(d_scaled, 0, keepdims=True)
        slope = jnp.mean(d_scaled * scaled, 0, keepdims=True)
        d_x = low16((center - scaled * slope) * rate)
        rows = code >> 16
        where = (code >> 8) & 255
        chosen = hot(jnp.broadcast_to(where, (CHUNK, width)) == iota((CHUNK, width), 0))
        d_place_ref[enc] += dot_last(d_x, chosen)
        wide = jnp.broadcast_to(rows, (CHUNK, width))

        def add(cut, carry):
            spot = pl.ds(pl.multiple_of(cut * CHUNK, CHUNK), CHUNK)
            chosen = hot(wide == iota((CHUNK, width), 0) + cut * CHUNK)
            d_table_ref[spot, :] += dot_last(chosen, d_x)
            return carry

        lax.fori_loop(0, sizes.padded // CHUNK, add, 0, unroll=not short)

    for enc in range(2):
        if sizes.keep:
            for copy in loads[2 * enc : 2 * enc + 2]:
                copy.wait()

            def kept_spans(turn, carry):
                steps = [turn * sizes.unroll[enc] + u for u in range(sizes.unroll[enc])]
                ats = [s if enc == 0 else sizes.steps[0] + s for s in steps]
                work(
                    enc,
                    steps,
                    [entry_ref[at, 0:1, :] for at in ats],
                    [kept_ref[at, 0:128, :] for at in ats],
                    [kept_ref[at, 128:129, :] for at in ats],
                )
                return carry

            lax.fori_loop(0, sizes.steps[enc] // sizes.unroll[enc], kept_spans, 0)

        def more_level(level, carry_level):
            def one_span(step, carry):
                code = pack_span(sizes, enc, step, level, first, raw_ref)[0]
                scaled, rate = gather_span(sizes, enc, code, table_t, place_t, True)
                work(enc, [step], [code], [scaled], [rate], True)
                return carry

            return lax.fori_loop(0, sizes.steps[enc], one_span, carry_level)

        lax.fori_loop(begin, levels_ref[0], more_level, 0)

    for step in range(sizes.steps[0]):
        d_query_ref[step * 8 : step * 8 + 8, 0:count_q, :] = low16(d_query_q[step]).reshape(8, count_q, 128)
    d_query_ref[:, count_q:, :] = low16(d_query_p[...])
    for enc in range(2):
        for part, block in enumerate((d_place_ref, d_attn_ref)):
            for cut in range(2):
                slice_ref[enc, 2 * part + cut] = block[enc, :, cut * 128 : (cut + 1) * 128].astype(
                    slice_ref.dtype
                )
    slice_ref[0, 1] = jnp.zeros_like(slice_ref[0, 1])
    sums = []
    same = iota((128, 128), 0) == iota((128, 128), 1)
    for enc in range(2):
        for row, acc in enumerate((acc_gain, acc_shift, acc_value)):
            tall = jnp.broadcast_to(jnp.sum(acc[enc], 1, keepdims=True), (128, 128))
            sums.append(jnp.sum(jnp.where(same, tall, 0.0), 0, keepdims=True))
    sums = jnp.concatenate(sums + [jnp.zeros((10, 128), jnp.float32)], 0)
    slice_ref[0, 1, 0:16, :] = sums.astype(slice_ref.dtype)


def tokens_backward(sizes, levels, every, query, mixed, lse, grad, kept, entry, table, positions, attention, vectors):
    many = sizes.many
    count_p = sizes.count[1]
    both = sum(sizes.count)
    return local_call(
        functools.partial(backward_kernel, sizes),
        (
            jax.ShapeDtypeStruct((many, both, 128), jnp.bfloat16),
            jax.ShapeDtypeStruct((sizes.padded, 128), jnp.float32),
            jax.ShapeDtypeStruct((2, 4, 128, 128), sizes.kind),
        ),
        (levels, every, query, mixed, lse, grad, kept, entry, table, positions, attention, vectors),
        token_scratch(sizes)
        + [
            pltpu.VMEM((2, 128, CHUNK), jnp.float32),
            pltpu.VMEM((2, 128, 256), jnp.float32),
            pltpu.VMEM((2, 128, SPAN), jnp.float32),
            pltpu.VMEM((2, 128, SPAN), jnp.float32),
            pltpu.VMEM((2, 128, SPAN), jnp.float32),
            pltpu.VMEM((sizes.steps[0], sizes.queries[0], 128), jnp.float32),
            pltpu.VMEM((many, count_p, 128), jnp.float32),
        ]
        + kept_scratch(sizes),
        "tokens_backward",
        smem_in=(0,),
        any_in=(6, 7),
    )


def adam(weight, grad, first, second):
    first_new = BETA_ONE * first + (1.0 - BETA_ONE) * grad
    second_new = BETA_TWO * second + (1.0 - BETA_TWO) * grad * grad
    fix_one = 1.0 - BETA_ONE**STEP
    fix_two = 1.0 - BETA_TWO**STEP
    ratio = first_new / fix_one / (jnp.sqrt(second_new / fix_two) + ADAM_EPS)
    return (first_new, second_new, weight - INNER_RATE * (ratio + WEIGHT_DECAY * weight))


def pieces_of(depth):
    blocks = [(1, (enc,)) for enc in range(2)] + [(2, (enc,)) for enc in range(2)]
    blocks += [(3, (enc, side)) for enc in range(2) for side in range(2)]
    return blocks + [(4, ())]


def square_sum(values):
    return jnp.sum(jnp.sum(values * values, 0, keepdims=True), 1, keepdims=True)


def finish_kernel(sizes, *refs):
    many = sizes.many
    count_q, count_p = sizes.count
    depth = sizes.depth
    (query_ref, slice_ref, d_table_ref, rows_ref, raw_ref, xa_q, xa_p, d_out, d_ffn, d_mid) = refs[:10]
    place_ref, attn_ref, vec_ref = refs[10:13]
    state = refs[13:33]
    norm_ref, g_word, g_place, g_attn, g_vec = refs[33:38]
    joined = refs[38:43]
    held = refs[43:63]
    mine = refs[63:68]
    theirs = refs[68:73]
    (query_all, slice_all, scalar_all, land_query, land_slice, own_query, own_slice, tile, table_t) = refs[73:82]
    send, recv, load, pair_send, pair_recv = refs[82:87]
    loads = []
    for index in range(20):
        copy = pltpu.make_async_copy(state[index], held[index], load.at[index])
        copy.start()
        loads.append(copy)
    me = lax.axis_index("dp")
    other = 1 - lax.axis_index("grp")
    barrier = pltpu.get_barrier_semaphore()

    def greet(step, carry):
        peer = lax.rem(me + step, many)
        pl.semaphore_signal(barrier, inc=1, device_id={"dp": peer}, device_id_type=MESH)
        return carry

    lax.fori_loop(1, many, greet, 0)
    pl.semaphore_signal(barrier, inc=1, device_id={"grp": other}, device_id_type=MESH)
    pl.semaphore_wait(barrier, many)
    query_pairs = [(lambda peer: query_ref.at[peer], land_query)]
    slice_pairs = [(lambda peer: slice_ref.at[peer], land_slice)]
    spread_start(many, me, query_pairs, send, recv, 0)
    spread_start(many, me, slice_pairs, send, recv, 1)
    land_query[me] = query_ref[me]
    land_slice[me] = slice_ref[me]
    spread_wait(many, me, query_pairs, send, recv, 0)
    own_query[...] = low16(jnp.sum(land_query[...].astype(jnp.float32), 0))
    query_back = [(lambda peer: own_query, query_all)]
    spread_start(many, me, query_back, send, recv, 3)
    query_all[me] = own_query[...]
    spread_wait(many, me, slice_pairs, send, recv, 1)
    own_slice[...] = jnp.sum(land_slice[...].astype(jnp.float32), 0).astype(own_slice.dtype)
    slice_back = [(lambda peer: own_slice, slice_all)]
    spread_start(many, me, slice_back, send, recv, 4)
    slice_all[me] = own_slice[...]
    spread_wait(many, me, query_back, send, recv, 3)

    g_vec[...] = d_mid[...]
    tops = []
    first = me * depth
    table_t[...] = jnp.zeros_like(table_t)
    rest = jnp.zeros((1, 1), jnp.float32)
    places = []
    for enc in range(2):
        low, high = (0, count_q) if enc == 0 else (count_q, count_q + count_p)
        number = many * (high - low)
        d_query = query_all[:, low:high, :].reshape(number, 128)
        x = rows_ref[:, low:high, :].reshape(number, 128).astype(jnp.float32) + place_ref[0, enc, 0:1, :]
        center = x - jnp.mean(x, -1, keepdims=True)
        rate = lax.rsqrt(jnp.mean(center * center, -1, keepdims=True) + NORM_EPS)
        scaled = center * rate
        gain = vector_row(vec_ref, enc, 0)
        a_low = low16(scaled * gain + vector_row(vec_ref, enc, 1))
        xa = xa_q if enc == 0 else xa_p
        d_h = xa[...] + dot_last(d_query, low16(attn_ref[0, enc, :, 0:128]))
        d_scaled = d_h * gain
        slope = jnp.mean(d_scaled * scaled, -1, keepdims=True)
        d_x = (d_scaled - jnp.mean(d_scaled, -1, keepdims=True) - scaled * slope) * rate
        d_place = jnp.sum(d_x, 0, keepdims=True)
        places.append(d_place)
        g_attn[enc, :, 0:128] = dot_rows(a_low, d_query)
        g_attn[enc, :, 384:512] = d_out[enc]
        spot = slice(enc, enc + 1)
        g_vec[2, spot, :] = jnp.sum(d_query.astype(jnp.float32), 0, keepdims=True)
        tops.append((jnp.sum(d_h * scaled, 0, keepdims=True), jnp.sum(d_h, 0, keepdims=True)))
        if enc == 0:
            columns = [
                part
                for peer in range(many)
                for part in (
                    raw_ref[peer, RAW_Q : RAW_Q + 16, 0:1].astype(jnp.int32)[0 : count_q // 2],
                    raw_ref[peer, RAW_Q : RAW_Q + 16, 64:65].astype(jnp.int32)[0 : count_q // 2],
                )
            ]
        else:
            columns = [raw_ref[peer, 0:count_p, 0:1].astype(jnp.int32) for peer in range(many)]
        spot = jnp.concatenate(columns, 0) - first
        spot = jnp.where(spot < depth, spot, -1)
        d_low = low16(d_x)
        wide = jnp.broadcast_to(spot, (number, CHUNK))
        for cut in range(sizes.padded // CHUNK):
            chosen = hot(wide == iota((number, CHUNK), 1) + cut * CHUNK)
            table_t[:, cut * CHUNK : (cut + 1) * CHUNK] += dot_rows(d_low, chosen)
        rest += square_sum(d_ffn[enc, 0]) + square_sum(d_ffn[enc, 1])
    for cut in range(0, depth, 128):
        top = min(cut + 128, depth)
        g_word[cut:top, :] = d_table_ref[cut:top, :] + jnp.transpose(table_t[:, cut : cut + 128])[0 : top - cut]
    tile[...] = jnp.broadcast_to(square_sum(g_word[...]), (8, 128))
    pairs = [(lambda peer: tile, scalar_all)]
    spread_start(many, me, pairs, send, recv, 5)
    scalar_all[me] = tile[...]
    spread_wait(many, me, slice_back, send, recv, 4)
    blocks = slice_all[...].astype(jnp.float32).reshape(8, 128, 128)
    for enc in range(2):
        spot = slice(enc, enc + 1)
        g_vec[0, spot, :] = blocks[1][enc * 3 : enc * 3 + 1] + tops[enc][0]
        g_vec[1, spot, :] = blocks[1][enc * 3 + 1 : enc * 3 + 2] + tops[enc][1]
        g_vec[3, spot, :] = blocks[1][enc * 3 + 2 : enc * 3 + 3]
        g_place[enc, 0:128, :] = jnp.transpose(blocks[enc * 4])
        if enc == 0:
            g_place[enc, 128:256, :] = jnp.zeros((128, 128), jnp.float32)
        else:
            g_place[enc, 128:256, :] = jnp.transpose(blocks[enc * 4 + 1])
        g_place[enc, 0:1, :] += places[enc]
        g_attn[enc, :, 128:256] = blocks[enc * 4 + 2]
        g_attn[enc, :, 256:384] = blocks[enc * 4 + 3]
        rest += square_sum(g_place[enc]) + square_sum(g_attn[enc])
    small = jnp.sum(g_vec[...] * g_vec[...], 0)
    rest += jnp.sum(jnp.sum(small, 0, keepdims=True), 1, keepdims=True)
    for copy in loads:
        copy.wait()
    spread_wait(many, me, pairs, send, recv, 5)
    norm = jnp.sqrt(jnp.sum(scalar_all[...], 0)[0:1, 0:1] + rest)
    norm_ref[...] = jnp.broadcast_to(norm, (8, 128))
    factor = CLIP_LIMIT / jnp.maximum(norm, CLIP_LIMIT)
    grads = (g_word, g_place, g_attn, d_ffn, g_vec)

    def differ(kind, at, rows):
        weight, moment, square, anchor = (held[kind * 4 + j] for j in range(4))
        grad = grads[kind][at + (rows,)] * factor
        inner = adam(weight[(0,) + at + (rows,)], grad, moment[(0,) + at + (rows,)], square[(0,) + at + (rows,)])[2]
        mine[kind][at + (rows,)] = (anchor[at + (rows,)] - inner).astype(mine[kind].dtype)

    size = math.gcd(depth, 128)

    def table_block(step, carry):
        differ(0, (), pl.ds(pl.multiple_of(step * size, size), size))
        return carry

    lax.fori_loop(0, depth // size, table_block, 0)
    ways = []

    def hand(kind):
        copy = pltpu.make_async_remote_copy(
            src_ref=mine[kind],
            dst_ref=theirs[kind],
            send_sem=pair_send.at[kind],
            recv_sem=pair_recv.at[kind],
            device_id={"grp": other},
            device_id_type=MESH,
        )
        copy.start()
        ways.append(copy)

    hand(0)
    for kind in range(1, 5):
        for found, at in pieces_of(depth):
            if found == kind:
                differ(kind, at, slice(0, 14) if kind == 4 else slice(None))
        hand(kind)
    def join(kind, spot):
        joined[kind][spot] = mine[kind][spot].astype(jnp.float32) + theirs[kind][spot].astype(jnp.float32)

    def table_add(step, carry):
        join(0, pl.ds(pl.multiple_of(step * size, size), size))
        return carry

    ways[0].wait()
    lax.fori_loop(0, depth // size, table_add, 0)
    for kind in range(1, 5):
        ways[kind].wait()
        for found, at in pieces_of(depth):
            if found == kind:
                join(kind, at if at else slice(None))


def finish(sizes, query, slices, d_table, rows, every, xa_q, xa_p, d_out, d_ffn, d_mid, params, state):
    many = sizes.many
    both = sum(sizes.count)
    inputs = (query, slices, d_table, rows, every, xa_q, xa_p, d_out, d_ffn, d_mid) + params
    flat = tuple(state[j][kind] for kind in range(5) for j in range(4))
    shapes = [state[3][kind].shape for kind in range(5)]
    vm = pl.BlockSpec(memory_space=pltpu.VMEM)
    hbm = pl.BlockSpec(memory_space=pl.ANY)
    f32 = jnp.float32
    return pl.pallas_call(
        functools.partial(finish_kernel, sizes),
        out_shape=tuple(
            jax.ShapeDtypeStruct(shape, f32)
            for shape in [(8, 128), shapes[0], shapes[1], shapes[2], (16, 2, 128)] + shapes
        ),
        in_specs=[vm] * len(inputs) + [hbm] * 20,
        out_specs=[vm] * 10,
        scratch_shapes=[pltpu.VMEM(value.shape, f32) for value in flat]
        + [pltpu.VMEM(shape, jnp.bfloat16 if kind < 4 else f32) for kind, shape in enumerate(shapes)] * 2
        + [
            pltpu.VMEM((many, both, 128), jnp.bfloat16),
            pltpu.VMEM((many, sizes.lines, 128), sizes.kind),
            pltpu.VMEM((many, 8, 128), f32),
            pltpu.VMEM((many, both, 128), jnp.bfloat16),
            pltpu.VMEM((many, sizes.lines, 128), sizes.kind),
            pltpu.VMEM((both, 128), jnp.bfloat16),
            pltpu.VMEM((sizes.lines, 128), sizes.kind),
            pltpu.VMEM((8, 128), f32),
            pltpu.VMEM((128, sizes.padded), f32),
            pltpu.SemaphoreType.DMA((6, many)),
            pltpu.SemaphoreType.DMA((6, many)),
            pltpu.SemaphoreType.DMA((20,)),
            pltpu.SemaphoreType.DMA((5,)),
            pltpu.SemaphoreType.DMA((5,)),
        ],
        compiler_params=pltpu.CompilerParams(
            collective_id=3, has_side_effects=True, vmem_limit_bytes=VMEM_LIMIT
        ),
        name="finish",
    )(*inputs, *flat)


def output_parts(depth):
    rows = depth // 3 if depth % 24 == 0 else depth
    parts = [(0, slice(at, at + rows)) for at in range(0, depth, rows)]
    return parts + [(kind, None) for kind in (3, 2, 1, 4)]


def outputs_kernel(depth, groups, *refs):
    norm_ref, g_vec = refs[:2]
    ins = refs[2:31]
    outs = refs[31:56]
    total_ref = refs[56]
    held = refs[57:86]
    made = refs[86:111]
    load, store = refs[111:113]
    parts = output_parts(depth)
    loads, stores = ([], [])
    for number, (kind, rows) in enumerate(parts):
        group = []
        for j in range(6 if kind < 4 else 5):
            index = kind * 5 + j if j < 5 else 25 + kind
            source, target = (ins[index], held[index])
            if rows is not None:
                lead = (0,) if len(source.shape) == 3 else ()
                source, target = (source.at[lead + (rows,)], target.at[lead + (rows,)])
            copy = pltpu.make_async_copy(source, target, load.at[number, j])
            copy.start()
            group.append(copy)
        loads.append(group)
    total_ref[0] = jnp.max(norm_ref[...])
    norm = norm_ref[0:1, 0:1]
    factor = CLIP_LIMIT / jnp.maximum(norm, CLIP_LIMIT)
    grads = tuple(held[25:29]) + (g_vec,)

    def work(kind, at, rows):
        moment, square, anchor, outer, summed = (held[kind * 5 + j] for j in range(5))
        first, second, average, momentum, weight = (made[kind * 5 + j] for j in range(5))
        spot = at + (rows,)
        deep = (0,) + spot
        grad = grads[kind][spot] * factor
        first[deep] = BETA_ONE * moment[deep] + (1.0 - BETA_ONE) * grad
        second[deep] = BETA_TWO * square[deep] + (1.0 - BETA_TWO) * grad * grad
        mean = summed[spot] / groups
        speed = OUTER_MU * outer[spot] + mean
        average[spot] = mean
        momentum[spot] = speed
        weight[deep] = anchor[spot] - OUTER_RATE * (mean + OUTER_MU * speed)

    for number, (kind, rows) in enumerate(parts):
        for copy in loads[number]:
            copy.wait()
        if kind == 0:
            size = math.gcd(rows.stop - rows.start, 128)

            def table_block(step, carry):
                work(0, (), pl.ds(pl.multiple_of(rows.start + step * size, size), size))
                return carry

            lax.fori_loop(0, (rows.stop - rows.start) // size, table_block, 0)
        else:
            for found, at in pieces_of(depth):
                if found == kind:
                    work(kind, at, slice(0, 14) if kind == 4 else slice(None))
        for j in range(5):
            source, target = (made[kind * 5 + j], outs[kind * 5 + j])
            if rows is not None:
                lead = (0,) if len(source.shape) == 3 else ()
                source, target = (source.at[lead + (rows,)], target.at[lead + (rows,)])
            copy = pltpu.make_async_copy(source, target, store.at[number, j])
            copy.start()
            stores.append(copy)
    for copy in stores:
        copy.wait()


def make_outputs(norm, grads, firsts, seconds, anchors, outers, summed, groups):
    kinds = range(5)
    flat = tuple(v for kind in kinds for v in (firsts[kind], seconds[kind], anchors[kind], outers[kind], summed[kind]))
    flat += tuple(grads[:4])
    out = tuple(
        jax.ShapeDtypeStruct(shape, jnp.float32)
        for kind in kinds
        for shape in (firsts[kind].shape, firsts[kind].shape, anchors[kind].shape, anchors[kind].shape, firsts[kind].shape)
    )
    vm = pl.BlockSpec(memory_space=pltpu.VMEM)
    hbm = pl.BlockSpec(memory_space=pl.ANY)
    got = pl.pallas_call(
        functools.partial(outputs_kernel, anchors[0].shape[0], groups),
        out_shape=out + (jax.ShapeDtypeStruct((1,), jnp.float32),),
        in_specs=[vm] * 2 + [hbm] * 29,
        out_specs=[hbm] * 25 + [pl.BlockSpec(memory_space=pltpu.SMEM)],
        scratch_shapes=[pltpu.VMEM(v.shape, jnp.float32) for v in flat]
        + [pltpu.VMEM(v.shape, jnp.float32) for v in out]
        + [pltpu.SemaphoreType.DMA((7, 6)), pltpu.SemaphoreType.DMA((7, 5))],
        compiler_params=pltpu.CompilerParams(vmem_limit_bytes=VMEM_LIMIT),
        name="make_outputs",
    )(norm, grads[4], *flat)
    return [[got[kind * 5 + j] for kind in kinds] for j in range(5)], got[25]


def square_norm(values):
    center = values - jnp.mean(values, -1, keepdims=True)
    rate = lax.rsqrt(jnp.mean(center * center, -1, keepdims=True) + NORM_EPS)
    return center * rate, rate


def norm_back(d_scaled, scaled, rate):
    slope = jnp.mean(d_scaled * scaled, -1, keepdims=True)
    return (d_scaled - jnp.mean(d_scaled, -1, keepdims=True) - scaled * slope) * rate


def total_of(values):
    return jnp.sum(jnp.sum(values, 0, keepdims=True), 1, keepdims=True)


def score_terms(scores, drop, target, weight, count, axis):
    masked = jnp.where(drop, MASKED, scores)
    top = jnp.max(masked, axis, keepdims=True)
    expo = jnp.exp(masked - top)
    total = jnp.sum(expo, axis, keepdims=True)
    picked = jnp.sum(jnp.where(target, scores, 0.0), axis, keepdims=True)
    loss = total_of(weight * (top + jnp.log(total) - picked))
    grad = low16((weight / count) * (expo / total - jnp.where(target, 1.0, 0.0)))
    return grad, loss


GELU_A = math.sqrt(2.0 / math.pi)
GELU_B = 0.044715


def class_kernel(
    sizes,
    rows_ref,
    mixed_ref,
    raw_ref,
    place_ref,
    attn_ref,
    ffn_ref,
    vec_ref,
    grad_ref,
    xa_q,
    xa_p,
    d_out,
    d_ffn,
    d_mid,
    loss_ref,
    count_ref,
    cls_ref,
    scaled_a,
    rate_a,
    scaled_f,
    rate_f,
    pre_ref,
    act_ref,
    low_ref,
    flag_ref,
):
    many = sizes.many
    counts = sizes.count
    totals = (many * counts[0], many * counts[1])
    chunk = totals[0]
    parts = [(0, 0, 0)] + [(1, at, totals[0] + at) for at in range(0, totals[1], chunk)]

    def held(ref, enc, at):
        each = counts[enc]
        low = 0 if enc == 0 else counts[0]
        return ref[at // each : (at + chunk) // each, low : low + each, :].reshape(chunk, 128)

    def weights(enc):
        return (
            low16(attn_ref[0, enc, :, 384:512]),
            low16(ffn_ref[0, enc, 0]),
            low16(ffn_ref[0, enc, 1]),
        )

    for enc, at, spot in parts:
        w_out, w_up, w_down = weights(enc)
        row = functools.partial(vector_row, vec_ref, enc)
        here = slice(spot, spot + chunk)
        x = held(rows_ref, enc, at).astype(jnp.float32) + place_ref[0, enc, 0:1, :]
        h_embed = norm_rows(x, row(0), row(1))
        scaled, rate = square_norm(h_embed + (dot(held(mixed_ref, enc, at), w_out) + row(4)))
        scaled_a[here, :] = scaled
        rate_a[here, :] = jnp.broadcast_to(rate, (chunk, 128))
        h_attn = scaled * row(5) + row(6)
        h_low = low16(h_attn)
        low_ref[here, :] = h_low
        pre = dot(h_low, w_up) + jnp.concatenate([row(10), row(11), row(12), row(13)], 1)
        pre_ref[here, :] = pre
        act = low16(0.5 * pre * (1.0 + jnp.tanh(GELU_A * (pre + GELU_B * (pre * pre * pre)))))
        act_ref[here, :] = act
        scaled, rate = square_norm(h_attn + (dot_last(act, w_down) + row(7)))
        scaled_f[here, :] = scaled
        rate_f[here, :] = jnp.broadcast_to(rate, (chunk, 128))
        cls_ref[here, :] = low16(scaled * row(8) + row(9))

    every_q = cls_ref[0 : totals[0], :]
    every_p = cls_ref[totals[0] :, :]
    flag_ref[...] = jnp.zeros_like(flag_ref)
    for peer in range(many):
        flag_ref[peer : peer + 1, :] = raw_ref[peer, RAW_Q:RAW_ROWS, :].astype(jnp.float32)[8:9]
    turned = jnp.transpose(flag_ref[...])

    def column(low, each):
        tall = jnp.concatenate([turned[low : low + each]] * many, 0)
        at = iota(tall.shape, 1) == iota(tall.shape, 0) // each
        return jnp.sum(jnp.where(at, tall, 0.0), 1, keepdims=True)

    keys_q = column(0, counts[0])
    valid = column(counts[0], counts[0])
    keys_p = column(2 * counts[0], counts[1])
    hot_q = hot(jnp.broadcast_to(keys_q, (totals[0], 128)) == iota((totals[0], 128), 1).astype(jnp.float32))
    hot_p = hot(jnp.broadcast_to(keys_p, (totals[1], 128)) == iota((totals[1], 128), 1).astype(jnp.float32))
    same = dot_last(hot_q, hot_p) > 0.5
    count = jnp.maximum(total_of(valid), 1.0)
    scale = 128 ** (-0.5)
    scores = dot_last(every_q, every_p) * scale
    index_q = iota(scores.shape, 0)
    index_p = iota(scores.shape, 1)
    target_qp = index_p == 2 * index_q
    target_pq = index_p // 2 == index_q
    grad_qp, loss_qp = score_terms(scores, same & ~target_qp, target_qp, valid, count, 1)
    drop_pq = (same | (jnp.broadcast_to(valid, scores.shape) == 0.0)) & ~target_pq
    weight_p = jnp.sum(jnp.where(target_qp, jnp.broadcast_to(valid, scores.shape), 0.0), 0, keepdims=True)
    grad_pq, loss_pq = score_terms(scores, drop_pq, target_pq, weight_p, count, 0)
    loss_ref[0] = jnp.max(loss_qp + loss_pq)
    count_ref[0] = jnp.max(count)
    d_q = (dot(grad_qp, every_p) + dot(grad_pq, every_p)) * scale
    d_p = (dot_rows(grad_pq, every_q) + dot_rows(grad_qp, every_q)) * scale

    d_mid[...] = jnp.zeros_like(d_mid)
    d_out[...] = jnp.zeros_like(d_out)
    d_ffn[...] = jnp.zeros_like(d_ffn)
    for enc, at, spot in parts:
        w_out, w_up, w_down = weights(enc)
        row = functools.partial(vector_row, vec_ref, enc)
        here = slice(spot, spot + chunk)

        def add(index, values):
            d_mid[index, enc : enc + 1, :] += jnp.sum(values, 0, keepdims=True)

        d_cls = d_q if enc == 0 else d_p[at : at + chunk]
        scaled = scaled_f[here, :]
        add(8, d_cls * scaled)
        add(9, d_cls)
        d_x_ffn = norm_back(d_cls * row(8), scaled, rate_f[here, :])
        d_branch = low16(d_x_ffn)
        add(7, d_branch.astype(jnp.float32))
        d_ffn[enc, 1] += dot_rows(d_branch, act_ref[here, :])
        d_act = dot(d_branch, w_down)
        pre = pre_ref[here, :]
        square = pre * pre
        bend = jnp.tanh(GELU_A * (pre + GELU_B * (square * pre)))
        slope = 0.5 * (1.0 + bend) + (0.5 * GELU_A) * pre * (1.0 - bend * bend) * (
            1.0 + (3.0 * GELU_B) * square
        )
        d_pre = low16(slope * d_act)
        up_bias = jnp.sum(d_pre.astype(jnp.float32), 0, keepdims=True)
        for cut in range(4):
            d_mid[10 + cut, enc : enc + 1, :] += up_bias[:, cut * 128 : (cut + 1) * 128]
        d_ffn[enc, 0] += dot_rows(low_ref[here, :], d_pre)
        d_h = d_x_ffn + dot_last(d_pre, w_up)
        scaled = scaled_a[here, :]
        add(5, d_h * scaled)
        add(6, d_h)
        d_x = norm_back(d_h * row(5), scaled, rate_a[here, :])
        if enc == 0:
            xa_q[...] = d_x
        else:
            xa_p[at : at + chunk, :] = d_x
        d_proj = low16(d_x)
        add(4, d_proj.astype(jnp.float32))
        d_out[enc] += dot_rows(held(mixed_ref, enc, at), d_proj)
        d_mixed = low16(dot_last(d_proj, w_out))
        each = counts[enc]
        low = 0 if enc == 0 else counts[0]
        grad_ref[at // each : (at + chunk) // each, low : low + each, :] = d_mixed.reshape(
            chunk // each, each, 128
        )


def class_stage(sizes, rows, mixed, every, positions, attention, feedforward, vectors):
    many = sizes.many
    n_q, n_p = (many * sizes.count[0], many * sizes.count[1])
    both = n_q + n_p
    f32 = jnp.float32
    return local_call(
        functools.partial(class_kernel, sizes),
        (
            jax.ShapeDtypeStruct((many, sum(sizes.count), 128), jnp.bfloat16),
            jax.ShapeDtypeStruct((n_q, 128), f32),
            jax.ShapeDtypeStruct((n_p, 128), f32),
            jax.ShapeDtypeStruct((2, 128, 128), f32),
            jax.ShapeDtypeStruct((2, 2, 128, 512), f32),
            jax.ShapeDtypeStruct((16, 2, 128), f32),
            jax.ShapeDtypeStruct((1,), f32),
            jax.ShapeDtypeStruct((1,), f32),
        ),
        (rows, mixed, every, positions, attention, feedforward, vectors),
        [
            pltpu.VMEM((both, 128), jnp.bfloat16),
            pltpu.VMEM((both, 128), f32),
            pltpu.VMEM((both, 128), f32),
            pltpu.VMEM((both, 128), f32),
            pltpu.VMEM((both, 128), f32),
            pltpu.VMEM((both, 512), f32),
            pltpu.VMEM((both, 512), jnp.bfloat16),
            pltpu.VMEM((both, 128), jnp.bfloat16),
            pltpu.VMEM((128, 128), f32),
        ],
        "class_stage",
        smem_out=(6, 7),
    )


def class_stage_large(sizes, rows_all, mixed_all, every, positions, attention, feedforward, vectors):
    many = sizes.many
    count_q, count_p = sizes.count
    counts = sizes.count
    width = rows_all.shape[2]
    flags_all = every[:, RAW_FLAGS, :].astype(jnp.int32)
    keys_q = flags_all[:, :count_q].reshape(-1)
    valid_all = flags_all[:, count_q : 2 * count_q].reshape(-1)
    keys_p = flags_all[:, 2 * count_q : 2 * count_q + count_p].reshape(-1)
    cuts = ((0, count_q), (count_q, count_q + count_p))
    cls, class_kept, mixes = ([], [], [])
    for enc in range(2):
        low, high = cuts[enc]
        rows = rows_all[:, low:high].reshape(-1, width)
        mixed = mixed_all[:, low:high].reshape(-1, width)
        low_cls, kept_cls = class_forward(
            rows, mixed, positions[0, enc], attention[0, enc], feedforward[0, enc], vectors[0, :, enc]
        )
        cls.append(low_cls)
        class_kept.append(kept_cls)
        mixes.append(mixed)
    d_q, d_p, loss_total, count = score_stage(cls[0], cls[1], keys_q, keys_p, valid_all)
    d_cls = (d_q, d_p)
    grads, xas, outs, ffns, mids = ([], [], [], [], [])
    for enc in range(2):
        d_mixed, d_x_attn, d_w_out, d_ffn, rows_mid, d_up_bias = class_backward(
            class_kept[enc], mixes[enc], attention[0, enc], feedforward[0, enc], vectors[0, :, enc], d_cls[enc]
        )
        grads.append(d_mixed.reshape(many, counts[enc], width))
        xas.append(d_x_attn)
        outs.append(d_w_out)
        ffns.append(d_ffn)
        mid = jnp.concatenate([jnp.stack(list(rows_mid)), d_up_bias.reshape(-1, width)])
        mids.append(jnp.pad(mid, ((4, 2), (0, 0))))
    return (
        jnp.concatenate(grads, 1),
        xas[0],
        xas[1],
        jnp.stack(outs),
        jnp.stack(ffns),
        jnp.stack(mids, 1),
        loss_total.reshape(1),
        count.reshape(1),
    )


def class_forward(rows, mixed, place, attn_w, ffn_w, vec):
    width = rows.shape[1]
    h_embed = layer_norm(rows.astype(jnp.float32) + place[:1], vec[0], vec[1])
    x_attn = h_embed + (dot(mixed, low16(attn_w[:, 3 * width :])) + vec[4])
    h_attn = layer_norm(x_attn, vec[5], vec[6])
    h_low = low16(h_attn)
    pre = dot(h_low, low16(ffn_w[0])) + vec[10:].reshape(-1)
    act = low16(gelu_tanh(pre))
    x_ffn = h_attn + (dot_last(act, low16(ffn_w[1])) + vec[7])
    h_out = layer_norm(x_ffn, vec[8], vec[9])
    return low16(h_out), (x_attn, h_low, pre, act, x_ffn)


def class_backward(kept, mixed, attn_w, ffn_w, vec, d_cls):
    x_attn, h_low, pre, act, x_ffn = kept
    width = x_attn.shape[1]
    unused, out_back = jax.vjp(layer_norm, x_ffn, vec[8], vec[9])
    d_x_ffn, d_gain_two, d_shift_two = out_back(d_cls)
    d_branch = low16(d_x_ffn)
    d_down_bias = jnp.sum(d_branch, 0, dtype=jnp.float32)
    d_down = dot_rows(d_branch, act)
    d_act = dot(d_branch, low16(ffn_w[1]))
    unused, gelu_back = jax.vjp(gelu_tanh, pre)
    d_pre = low16(gelu_back(d_act)[0])
    d_up_bias = jnp.sum(d_pre, 0, dtype=jnp.float32)
    d_up = dot_rows(h_low, d_pre)
    d_h_attn = d_x_ffn + dot_last(d_pre, low16(ffn_w[0]))
    unused, attn_back = jax.vjp(layer_norm, x_attn, vec[5], vec[6])
    d_x_attn, d_gain_one, d_shift_one = attn_back(d_h_attn)
    d_proj = low16(d_x_attn)
    d_out_bias = jnp.sum(d_proj, 0, dtype=jnp.float32)
    d_w_out = dot_rows(mixed, d_proj)
    d_mixed = low16(dot_last(d_proj, low16(attn_w[:, 3 * width :])))
    rows = (d_out_bias, d_gain_one, d_shift_one, d_down_bias, d_gain_two, d_shift_two)
    return d_mixed, d_x_attn, d_w_out, jnp.stack([d_up, d_down]), rows, d_up_bias


def softmax_terms(scores, drop, target, weight, count, axis):
    masked = jnp.where(drop, MASKED, scores)
    top = jnp.max(masked, axis, keepdims=True)
    expo = jnp.exp(masked - top)
    total = jnp.sum(expo, axis, keepdims=True)
    lse = top + jnp.log(total)
    picked = jnp.sum(jnp.where(target, scores, 0.0), axis, keepdims=True)
    loss = jnp.sum(weight * (lse - picked))
    grad = low16((weight / count) * (expo / total - target.astype(jnp.float32)))
    return grad, loss


def score_stage(every_q, every_p, keys_q, keys_p, valid_q):
    count = jnp.maximum(jnp.sum(valid_q).astype(jnp.float32), 1.0)
    scale = every_q.shape[1] ** (-0.5)
    index_q = jnp.arange(every_q.shape[0])[:, None]
    index_p = jnp.arange(every_p.shape[0])[None, :]
    scores = dot_last(every_q, every_p) * scale
    same = keys_q[:, None] == keys_p[None, :]
    target_qp = index_p == 2 * index_q
    valid = valid_q.astype(jnp.float32)[:, None]
    grad_qp, loss_qp = softmax_terms(scores, same & ~target_qp, target_qp, valid, count, 1)
    target_pq = index_p // 2 == index_q
    drop_pq = (same | (valid_q[:, None] == 0)) & ~target_pq
    owner_valid = jnp.repeat(valid_q, 2)
    weight_p = jnp.where(index_p[0] % 2 == 0, owner_valid, 0).astype(jnp.float32)[None, :]
    grad_pq, loss_pq = softmax_terms(scores, drop_pq, target_pq, weight_p, count, 0)
    d_q = (dot(grad_qp, every_p) + dot(grad_pq, every_p)) * scale
    d_p = (dot_rows(grad_pq, every_q) + dot_rows(grad_qp, every_q)) * scale
    return d_q, d_p, loss_qp + loss_pq, count


def body(
    question_ids,
    passage_ids,
    question_lengths,
    passage_lengths,
    question_keys,
    passage_keys,
    question_valid,
    word_table,
    positions,
    attention,
    feedforward,
    vectors,
    word_first,
    positions_first,
    attention_first,
    feedforward_first,
    vectors_first,
    word_second,
    positions_second,
    attention_second,
    feedforward_second,
    vectors_second,
    word_anchor,
    positions_anchor,
    attention_anchor,
    feedforward_anchor,
    vectors_anchor,
    word_outer,
    positions_outer,
    attention_outer,
    feedforward_outer,
    vectors_outer,
):
    many = lax.axis_size("dp")
    count_q = question_ids.shape[0]
    count_p = passage_ids.shape[0]
    table = word_table[0]
    sizes = Sizes(many, count_q, count_p, table.shape[0])
    swap = lambda values: jnp.swapaxes(values, -3, -2)
    vectors, vectors_first, vectors_second, vectors_anchor, vectors_outer = (
        swap(v) for v in (vectors, vectors_first, vectors_second, vectors_anchor, vectors_outer)
    )
    every, class_rows, kept, entry, counted = first_stage(
        sizes,
        question_ids,
        passage_ids,
        question_lengths,
        passage_lengths,
        question_keys,
        question_valid,
        passage_keys,
        table,
        positions,
    )
    part, lse_part, query, levels = tokens_forward(
        sizes, every, class_rows, kept, entry, counted, table, positions, attention, vectors
    )
    mixed_all, lse_all = exchange_mixed(sizes, part, lse_part)
    stage = class_stage if many * count_q <= 512 else class_stage_large
    grad_all, xa_q, xa_p, d_out, d_ffn, d_mid, loss_total, count = stage(
        sizes, class_rows, mixed_all, every, positions, attention, feedforward, vectors
    )
    d_query, d_table, slices = tokens_backward(
        sizes, levels, every, query, mixed_all, lse_all, grad_all, kept, entry, table, positions, attention, vectors
    )
    weights = (word_table, positions, attention, feedforward, vectors)
    firsts = (word_first, positions_first, attention_first, feedforward_first, vectors_first)
    seconds = (word_second, positions_second, attention_second, feedforward_second, vectors_second)
    anchors = (word_anchor, positions_anchor, attention_anchor, feedforward_anchor, vectors_anchor)
    outers = (word_outer, positions_outer, attention_outer, feedforward_outer, vectors_outer)
    done = finish(
        sizes,
        d_query,
        slices.reshape(many, sizes.lines, 128),
        d_table,
        class_rows,
        every,
        xa_q,
        xa_p,
        d_out,
        d_ffn,
        d_mid,
        (positions, attention, vectors),
        (weights, firsts, seconds, anchors),
    )
    norm = done[0]
    grads = (done[1], done[2], done[3], d_ffn, done[4])
    made, norm = make_outputs(
        norm, grads, firsts, seconds, anchors, outers, done[5:10], lax.axis_size("grp")
    )
    first_new, second_new, averages, outer_next, weight_next = (
        part[:4] + [swap(part[4])] for part in made
    )
    return (
        loss_total.reshape(1),
        count.reshape(1),
        norm.reshape(1),
        first_new[0],
        first_new[1],
        first_new[2],
        first_new[3],
        first_new[4],
        second_new[0],
        second_new[1],
        second_new[2],
        second_new[3],
        second_new[4],
        averages[0],
        averages[1],
        averages[2],
        averages[3],
        averages[4],
        outer_next[0],
        outer_next[1],
        outer_next[2],
        outer_next[3],
        outer_next[4],
        weight_next[0],
        weight_next[1],
        weight_next[2],
        weight_next[3],
        weight_next[4],
    )


def solution(mesh):
    placed = (
        P(("grp", "dp"), None),
        P(("grp", "dp"), None),
        P(("grp", "dp")),
        P(("grp", "dp")),
        P(("grp", "dp")),
        P(("grp", "dp")),
        P(("grp", "dp")),
        P("grp", "dp", None),
        P("grp", None, None, None),
        P("grp", None, None, None),
        P("grp", None, None, None, None),
        P("grp", None, None, None),
        P("grp", "dp", None),
        P("grp", None, None, None),
        P("grp", None, None, None),
        P("grp", None, None, None, None),
        P("grp", None, None, None),
        P("grp", "dp", None),
        P("grp", None, None, None),
        P("grp", None, None, None),
        P("grp", None, None, None, None),
        P("grp", None, None, None),
        P("dp", None),
        P(),
        P(),
        P(),
        P(),
        P("dp", None),
        P(),
        P(),
        P(),
        P(),
    )
    return jax.shard_map(
        body,
        mesh=mesh,
        in_specs=placed,
        out_specs=(
            P("grp"),
            P("grp"),
            P("grp"),
            P("grp", "dp", None),
            P("grp", None, None, None),
            P("grp", None, None, None),
            P("grp", None, None, None, None),
            P("grp", None, None, None),
            P("grp", "dp", None),
            P("grp", None, None, None),
            P("grp", None, None, None),
            P("grp", None, None, None, None),
            P("grp", None, None, None),
            P("dp", None),
            P(),
            P(),
            P(),
            P(),
            P("dp", None),
            P(),
            P(),
            P(),
            P(),
            P("grp", "dp", None),
            P("grp", None, None, None),
            P("grp", None, None, None),
            P("grp", None, None, None, None),
            P("grp", None, None, None),
        ),
        check_vma=False,
    )
```

profile of v0, /device:TPU:0, one launch (start us, length us, event | category | flops | bytes accessed | tf_op | source)
XLA Modules:
  0.0 158.9 jit_solution(16398857683941877813)
XLA Ops:
  0.7 39.2 %first_stage.1 = (s16[16,80,128]{2,1,0:T(8,128)(2,1)}, bf16[16,48,128]{2,1,0:T(8,128)(2,1)}, f32[18,136,512]{2,1,0:T(8,128)}, s32[18,8,512]{2,1,0:T(8,128)}, f32[8,128]{1,0:T(8,128)}) custom-call(s32[16,64]{1,0:T(8,128)} %question_ref.1, s32[32,256]{1,0:T(8,128)} %passage_ref.1, s32[16]{0:T(128)} %length_q.1, s32[32]{0:T(128)} %length_p.1, s32[16]{0:T(128)} %key_q.1, ...), custom_call_target="tpu_custom_call" | custom-call | tf_op jit(solution)/shard_map/first_stage/pallas_call | solution.py:275
  39.8 9.0 %tokens_forward.1 = (bf16[16,48,128]{2,1,0:T(8,128)(2,1)}, f32[16,2,128]{2,1,0:T(2,128)}, bf16[16,48,128]{2,1,0:T(8,128)(2,1)}, s32[1]{0:T(128)}) custom-call(s16[16,80,128]{2,1,0:T(8,128)(2,1)} %get-tuple-element.87.raw_ref.refs_4_, bf16[16,48,128]{2,1,0:T(8,128)(2,1)} %get-tuple-element.86.rows_ref.refs_3_, f32[18,136,512]{2,1,0:T(8,128)} %get-tuple-element.88.kept_hbm, ...), custom_call_target="tpu_custom_call" | custom-call | tf_op jit(solution)/shard_map/tokens_forward/pallas_call | solution.py:663
  48.9 22.8 %exchange_mixed.1 = (bf16[16,48,128]{2,1,0:T(8,128)(2,1)}, f32[16,2,128]{2,1,0:T(2,128)}) custom-call(bf16[16,48,128]{2,1,0:T(8,128)(2,1)} %get-tuple-element.91.part_ref, f32[16,2,128]{2,1,0:T(2,128)} %get-tuple-element.92.lse_ref), custom_call_target="tpu_custom_call" | custom-call | tf_op jit(solution)/shard_map/exchange_mixed/pallas_call | solution.py:738
  71.6 8.2 %class_stage.1 = (bf16[16,48,128]{2,1,0:T(8,128)(2,1)}, f32[256,128]{1,0:T(8,128)}, f32[512,128]{1,0:T(8,128)}, f32[2,128,128]{2,1,0:T(8,128)}, f32[2,2,128,512]...) custom-call(bf16[16,48,128]{2,1,0:T(8,128)(2,1)} %get-tuple-element.86.rows_ref.refs_3_, ...), custom_call_target="tpu_custom_call" | custom-call | tf_op jit(solution)/shard_map/class_stage/pallas_call | solution.py:663
  79.9 26.7 %tokens_backward.1 = (bf16[16,48,128]{2,1,0:T(8,128)(2,1)}, f32[2048,128]{1,0:T(8,128)}, bf16[2,4,128,128]{3,2,1,0:T(8,128)(2,1)}) custom-call(s32[1]{0:T(128)} %get-tuple-element.96.levels_ref, s16[16,80,128]{2,1,0:T(8,128)(2,1)} %get-tuple-element.87.raw_ref.refs_4_, bf16[16,48,128]{2,1,0:T(8,128)(2,1)} %get-tuple-element.97.query_ref, ...), custom_call_target="tpu_custom_call" | custom-call | tf_op jit(solution)/shard_map/tokens_backward/pallas_call | solution.py:663
  106.6 40.2 %finish.1 = (f32[8,128]{1,0:T(8,128)}, f32[1920,128]{1,0:T(8,128)}, f32[2,256,128]{2,1,0:T(8,128)}, f32[2,128,512]{2,1,0:T(8,128)}, f32[16,2,128]{2,1,0:T(2,128)...) custom-call(bf16[16,48,128]{2,1,0:T(8,128)(2,1)} %get-tuple-element., ...), custom_call_target="tpu_custom_call" | custom-call | tf_op jit(solution)/shard_map/finish/pallas_call | solution.py:1183
  146.7 12.0 %make_outputs.1 = (f32[1,1920,128]{2,1,0:T(8,128)}, f32[1,1920,128]{2,1,0:T(8,128)}, f32[1920,128]{1,0:T(8,128)}, f32[1920,128]{1,0:T(8,128)}, f32[1,1920,128]{2...) custom-call(f32[8,128]{1,0:T(8,128)} %get-tuple-element.108.refs_0_,, ...), custom_call_target="tpu_custom_call" | custom-call | tf_op jit(solution)/shard_map/make_outputs/pallas_call | solution.py:1301
where the time goes:
time: 159 us
  Pallas kernels  158 us (99%)
    pallas_call x3, Pallas kernels, local_call(): pl.pallas_call(kernel, out_shape=out_shape, in_specs=[sm if i in smem_in...  43.9 us
    pallas_call x1, Pallas kernels, finish(): pl.pallas_call(functools.partial(finish_kernel, sizes), out_shape=tuple((...  40.2 us
    pallas_call x1, Pallas kernels, first_stage(): pl.pallas_call(functools.partial(first_kernel, sizes), out_shape=(jax.Sha...  39.2 us
    pallas_call x1, Pallas kernels, remote_call(): pl.pallas_call(kernel, out_shape=out_shape, in_specs=[pl.BlockSpec(memory...  22.8 us
    pallas_call x1, Pallas kernels, make_outputs(): pl.pallas_call(functools.partial(outputs_kernel, anchors[0].shape[0], gro...  12 us

commit v1 on v0

--- a/solution.py
+++ b/solution.py
@@ -115,6 +115,122 @@
         return carry
 
     lax.fori_loop(1, many, step_wait, 0)
+
+
+NEAR = 4
+
+
+def place_of(many, me, far, near):
+    row = lax.rem(me // NEAR + far, many // NEAR)
+    return row * NEAR + lax.rem(lax.rem(me, NEAR) + near, NEAR)
+
+
+def relay_start(many, me, source, landing, send, recv, slot):
+    for near in range(NEAR):
+        count = many // NEAR if near == 0 else 1
+
+        def one(far, carry):
+            peer = place_of(many, me, far, near)
+            copy_to(peer, source, landing.at[me], send.at[slot, peer], recv.at[slot, me]).start()
+            return carry
+
+        lax.fori_loop(1 if near == 0 else 0, count, one, 0)
+
+
+def relay_pass(many, me, source, landing, send, recv, slot):
+    def one(far, carry):
+        block = place_of(many, me, far, 0)
+        copy_to(block, source, landing.at[block], send.at[slot, block], recv.at[slot, block]).wait_recv()
+        for near in range(1, NEAR):
+            peer = place_of(many, me, 0, near)
+            key = place_of(many, me, far, near)
+            copy_to(peer, landing.at[block], landing.at[block], send.at[slot, key], recv.at[slot, block]).start()
+        return carry
+
+    lax.fori_loop(1, many // NEAR, one, 0)
+
+
+def relay_wait(many, me, source, landing, send, recv, slot):
+    def one(far, carry):
+        for near in range(NEAR):
+            key = place_of(many, me, far, near)
+            copy = copy_to(key, source, landing.at[key], send.at[slot, key], recv.at[slot, key])
+
+            @pl.when((far > 0) | (near > 0))
+            def _():
+                copy.wait_send()
+
+            if near > 0:
+                copy.wait_recv()
+        return carry
+
+    lax.fori_loop(0, many // NEAR, one, 0)
+
+
+def fold_start(many, me, blocks, landing, send, recv, slot):
+    def one(row, carry):
+        for near in range(1, NEAR):
+            peer = place_of(many, me, 0, near)
+            target = row * NEAR + lax.rem(peer, NEAR)
+            copy_to(
+                peer,
+                blocks.at[target],
+                landing.at[row * NEAR + lax.rem(me, NEAR)],
+                send.at[slot, target],
+                recv.at[slot, row * NEAR + lax.rem(me, NEAR)],
+            ).start()
+        mine = row * NEAR + lax.rem(me, NEAR)
+        landing[mine] = blocks[mine]
+        return carry
+
+    lax.fori_loop(0, many // NEAR, one, 0)
+
+
+def fold_pass(many, me, blocks, landing, halves, second, send, recv, slot, later):
+    def one(row, carry):
+        for near in range(1, NEAR):
+            key = row * NEAR + lax.rem(place_of(many, me, 0, near), NEAR)
+            copy = copy_to(
+                place_of(many, me, 0, near), blocks.at[key], landing.at[key], send.at[slot, key], recv.at[slot, key]
+            )
+            copy.wait_recv()
+            copy.wait_send()
+        return carry
+
+    lax.fori_loop(0, many // NEAR, one, 0)
+
+    def two(far, carry):
+        peer = place_of(many, me, far, 0)
+        row = peer // NEAR
+        total = landing[row * NEAR].astype(jnp.float32)
+        for near in range(1, NEAR):
+            total += landing[row * NEAR + near].astype(jnp.float32)
+        halves[row] = total.astype(halves.dtype)
+
+        @pl.when(far > 0)
+        def _():
+            copy_to(peer, halves.at[row], second.at[me // NEAR], send.at[later, row], recv.at[later, me // NEAR]).start()
+
+        @pl.when(far == 0)
+        def _():
+            second[row] = halves[row]
+
+        return carry
+
+    lax.fori_loop(0, many // NEAR, two, 0)
+
+
+def fold_wait(many, me, halves, second, send, recv, later):
+    def one(far, carry):
+        peer = place_of(many, me, far, 0)
+        row = peer // NEAR
+        copy = copy_to(peer, halves.at[row], second.at[row], send.at[later, row], recv.at[later, row])
+        copy.wait_recv()
+        copy.wait_send()
+        return carry
+
+    lax.fori_loop(1, many // NEAR, one, 0)
+    return jnp.sum(second[...].astype(jnp.float32), 0)
 
 
 def dot(left, right):
@@ -235,8 +351,18 @@
         prepare_tokens(sizes, table_ref, place_ref, table_t, place_t)
     spread_wait(many, me, raw_pairs, send, recv, 1)
 
+    row_pairs = [(lambda peer: own, rows_ref)]
+
+    def send_rows():
+        spread_wait(many, me, offer_pairs, send, recv, 2)
+        own[...] = low16(jnp.sum(landed[...].astype(jnp.float32), 0))
+        spread_start(many, me, row_pairs, send, recv, 3)
+        rows_ref[me] = own[...]
+
     def spans_of(enc, count):
         def spans(turn, count):
+            if enc == 1:
+                pl.when(turn == 1)(send_rows)
             steps = [turn * sizes.unroll[enc] + u for u in range(sizes.unroll[enc])]
             packed = [pack_span(sizes, enc, s, 0, first, every_ref) for s in steps]
             found = [gather_span(sizes, enc, part[0], table_t, place_t) for part in packed]
@@ -253,14 +379,9 @@
 
     count = jnp.zeros((8, 128), jnp.float32)
     if sizes.keep:
-        count = spans_of(0, count)
-    spread_wait(many, me, offer_pairs, send, recv, 2)
-    own[...] = low16(jnp.sum(landed[...].astype(jnp.float32), 0))
-    row_pairs = [(lambda peer: own, rows_ref)]
-    spread_start(many, me, row_pairs, send, recv, 3)
-    rows_ref[me] = own[...]
-    if sizes.keep:
-        count = spans_of(1, count)
+        count = spans_of(1, spans_of(0, count))
+    else:
+        send_rows()
     count_ref[...] = count
     spread_wait(many, me, row_pairs, send, recv, 3)
 
@@ -334,6 +455,7 @@
         self.spans = self.steps[0] + self.steps[1]
         self.devices = (2 * WAYS, 1)
         self.queries = (2 * WAYS * count_q, count_p)
+        assert self.steps[1] // self.unroll[1] > 1
         self.lines = 1024 // many
         self.kind = jnp.bfloat16 if self.lines % 16 == 0 else jnp.float32
         self.keep = self.spans * 136 * SPAN * 4 <= 8 * 1024 * 1024
@@ -1006,7 +1128,8 @@
     mine = refs[63:68]
     theirs = refs[68:73]
     (query_all, slice_all, scalar_all, land_query, land_slice, own_query, own_slice, tile, table_t) = refs[73:82]
-    send, recv, load, pair_send, pair_recv = refs[82:87]
+    half_query, far_query, half_slice, far_slice = refs[82:86]
+    send, recv, load, pair_send, pair_recv = refs[86:91]
     loads = []
     for index in range(20):
         copy = pltpu.make_async_copy(state[index], held[index], load.at[index])
@@ -1024,23 +1147,19 @@
     lax.fori_loop(1, many, greet, 0)
     pl.semaphore_signal(barrier, inc=1, device_id={"grp": other}, device_id_type=MESH)
     pl.semaphore_wait(barrier, many)
-    query_pairs = [(lambda peer: query_ref.at[peer], land_query)]
-    slice_pairs = [(lambda peer: slice_ref.at[peer], land_slice)]
-    spread_start(many, me, query_pairs, send, recv, 0)
-    spread_start(many, me, slice_pairs, send, recv, 1)
-    land_query[me] = query_ref[me]
-    land_slice[me] = slice_ref[me]
-    spread_wait(many, me, query_pairs, send, recv, 0)
-    own_query[...] = low16(jnp.sum(land_query[...].astype(jnp.float32), 0))
-    query_back = [(lambda peer: own_query, query_all)]
-    spread_start(many, me, query_back, send, recv, 3)
+    fold_start(many, me, query_ref, land_query, send, recv, 0)
+    fold_start(many, me, slice_ref, land_slice, send, recv, 1)
+    fold_pass(many, me, query_ref, land_query, half_query, far_query, send, recv, 0, 6)
+    fold_pass(many, me, slice_ref, land_slice, half_slice, far_slice, send, recv, 1, 7)
+    own_query[...] = low16(fold_wait(many, me, half_query, far_query, send, recv, 6))
+    relay_start(many, me, own_query, query_all, send, recv, 3)
     query_all[me] = own_query[...]
-    spread_wait(many, me, slice_pairs, send, recv, 1)
-    own_slice[...] = jnp.sum(land_slice[...].astype(jnp.float32), 0).astype(own_slice.dtype)
-    slice_back = [(lambda peer: own_slice, slice_all)]
-    spread_start(many, me, slice_back, send, recv, 4)
+    own_slice[...] = fold_wait(many, me, half_slice, far_slice, send, recv, 7).astype(own_slice.dtype)
+    relay_start(many, me, own_slice, slice_all, send, recv, 4)
     slice_all[me] = own_slice[...]
-    spread_wait(many, me, query_back, send, recv, 3)
+    relay_pass(many, me, own_query, query_all, send, recv, 3)
+    relay_pass(many, me, own_slice, slice_all, send, recv, 4)
+    relay_wait(many, me, own_query, query_all, send, recv, 3)
 
     g_vec[...] = d_mid[...]
     tops = []
@@ -1096,7 +1215,7 @@
     pairs = [(lambda peer: tile, scalar_all)]
     spread_start(many, me, pairs, send, recv, 5)
     scalar_all[me] = tile[...]
-    spread_wait(many, me, slice_back, send, recv, 4)
+    relay_wait(many, me, own_slice, slice_all, send, recv, 4)
     blocks = slice_all[...].astype(jnp.float32).reshape(8, 128, 128)
     for enc in range(2):
         spot = slice(enc, enc + 1)
@@ -1200,8 +1319,12 @@
             pltpu.VMEM((sizes.lines, 128), sizes.kind),
             pltpu.VMEM((8, 128), f32),
             pltpu.VMEM((128, sizes.padded), f32),
-            pltpu.SemaphoreType.DMA((6, many)),
-            pltpu.SemaphoreType.DMA((6, many)),
+            pltpu.VMEM((many // NEAR, both, 128), jnp.bfloat16),
+            pltpu.VMEM((many // NEAR, both, 128), jnp.bfloat16),
+            pltpu.VMEM((many // NEAR, sizes.lines, 128), sizes.kind),
+            pltpu.VMEM((many // NEAR, sizes.lines, 128), sizes.kind),
+            pltpu.SemaphoreType.DMA((8, many)),
+            pltpu.SemaphoreType.DMA((8, many)),
             pltpu.SemaphoreType.DMA((20,)),
             pltpu.SemaphoreType.DMA((5,)),
             pltpu.SemaphoreType.DMA((5,)),

time: 159 us -> 156 us (0.981)
  Pallas kernels: 158 us -> 154 us
    pallas_call x1, Pallas kernels: 40.2 us -> 36.4 us  [finish(): pl.pallas_call(functools.partial(finish_kernel, sizes), out_shape=tuple((...]
    pallas_call x1, Pallas kernels: 22.8 us -> 24.8 us  [remote_call(): pl.pallas_call(kernel, out_shape=out_shape, in_specs=[pl.BlockSpec(memory...]
    pallas_call x1, Pallas kernels: 39.2 us -> 37.2 us  [first_stage(): pl.pallas_call(functools.partial(first_kernel, sizes), out_shape=(jax.Sha...]
where the time goes in v1:
time: 156 us; the launch traced here: 155 us
  Pallas kernels  154 us (99%)
    pallas_call x3, Pallas kernels, local_call(): pl.pallas_call(kernel, out_shape=out_shape, in_specs=[sm if i in smem_in...  43.9 us
    pallas_call x1, Pallas kernels, first_stage(): pl.pallas_call(functools.partial(first_kernel, sizes), out_shape=(jax.Sha...  37.2 us
    pallas_call x1, Pallas kernels, finish(): pl.pallas_call(functools.partial(finish_kernel, sizes), out_shape=tuple((...  36.4 us
    pallas_call x1, Pallas kernels, remote_call(): pl.pallas_call(kernel, out_shape=out_shape, in_specs=[pl.BlockSpec(memory...  24.8 us
    pallas_call x1, Pallas kernels, make_outputs(): pl.pallas_call(functools.partial(outputs_kernel, anchors[0].shape[0], gro...  12 us

profile of v1, /device:TPU:0, one launch (start us, length us, event | category | flops | bytes accessed | tf_op | source)
XLA Modules:
  0.0 155.2 jit_solution(10183410205171816543)
XLA Ops:
  0.7 37.2 %first_stage.1 = (s16[16,80,128]{2,1,0:T(8,128)(2,1)}, bf16[16,48,128]{2,1,0:T(8,128)(2,1)}, f32[18,136,512]{2,1,0:T(8,128)}, s32[18,8,512]{2,1,0:T(8,128)}, f32[8,128]{1,0:T(8,128)}) custom-call(s32[16,64]{1,0:T(8,128)} %question_ref.1, s32[32,256]{1,0:T(8,128)} %passage_ref.1, s32[16]{0:T(128)} %length_q.1, s32[32]{0:T(128)} %length_p.1, s32[16]{0:T(128)} %key_q.1, ...), custom_call_target="tpu_custom_call" | custom-call | tf_op jit(solution)/shard_map/first_stage/pallas_call | solution.py:396
  37.8 9.0 %tokens_forward.1 = (bf16[16,48,128]{2,1,0:T(8,128)(2,1)}, f32[16,2,128]{2,1,0:T(2,128)}, bf16[16,48,128]{2,1,0:T(8,128)(2,1)}, s32[1]{0:T(128)}) custom-call(s16[16,80,128]{2,1,0:T(8,128)(2,1)} %get-tuple-element.87.raw_ref.refs_4_, bf16[16,48,128]{2,1,0:T(8,128)(2,1)} %get-tuple-element.86.rows_ref.refs_3_, f32[18,136,512]{2,1,0:T(8,128)} %get-tuple-element.88.kept_hbm, ...), custom_call_target="tpu_custom_call" | custom-call | tf_op jit(solution)/shard_map/tokens_forward/pallas_call | solution.py:785
  46.8 24.8 %exchange_mixed.1 = (bf16[16,48,128]{2,1,0:T(8,128)(2,1)}, f32[16,2,128]{2,1,0:T(2,128)}) custom-call(bf16[16,48,128]{2,1,0:T(8,128)(2,1)} %get-tuple-element.91.part_ref, f32[16,2,128]{2,1,0:T(2,128)} %get-tuple-element.92.lse_ref), custom_call_target="tpu_custom_call" | custom-call | tf_op jit(solution)/shard_map/exchange_mixed/pallas_call | solution.py:860
  71.7 8.2 %class_stage.1 = (bf16[16,48,128]{2,1,0:T(8,128)(2,1)}, f32[256,128]{1,0:T(8,128)}, f32[512,128]{1,0:T(8,128)}, f32[2,128,128]{2,1,0:T(8,128)}, f32[2,2,128,512]...) custom-call(bf16[16,48,128]{2,1,0:T(8,128)(2,1)} %get-tuple-element.86.rows_ref.refs_3_, ...), custom_call_target="tpu_custom_call" | custom-call | tf_op jit(solution)/shard_map/class_stage/pallas_call | solution.py:785
  79.9 26.7 %tokens_backward.1 = (bf16[16,48,128]{2,1,0:T(8,128)(2,1)}, f32[2048,128]{1,0:T(8,128)}, bf16[2,4,128,128]{3,2,1,0:T(8,128)(2,1)}) custom-call(s32[1]{0:T(128)} %get-tuple-element.96.levels_ref, s16[16,80,128]{2,1,0:T(8,128)(2,1)} %get-tuple-element.87.raw_ref.refs_4_, bf16[16,48,128]{2,1,0:T(8,128)(2,1)} %get-tuple-element.97.query_ref, ...), custom_call_target="tpu_custom_call" | custom-call | tf_op jit(solution)/shard_map/tokens_backward/pallas_call | solution.py:785
  106.6 36.4 %finish.1 = (f32[8,128]{1,0:T(8,128)}, f32[1920,128]{1,0:T(8,128)}, f32[2,256,128]{2,1,0:T(8,128)}, f32[2,128,512]{2,1,0:T(8,128)}, f32[16,2,128]{2,1,0:T(2,128)...) custom-call(bf16[16,48,128]{2,1,0:T(8,128)(2,1)} %get-tuple-element., ...), custom_call_target="tpu_custom_call" | custom-call | tf_op jit(solution)/shard_map/finish/pallas_call | solution.py:1302
  143.0 12.0 %make_outputs.1 = (f32[1,1920,128]{2,1,0:T(8,128)}, f32[1,1920,128]{2,1,0:T(8,128)}, f32[1920,128]{1,0:T(8,128)}, f32[1920,128]{1,0:T(8,128)}, f32[1,1920,128]{2...) custom-call(f32[8,128]{1,0:T(8,128)} %get-tuple-element.108.refs_0_,, ...), custom_call_target="tpu_custom_call" | custom-call | tf_op jit(solution)/shard_map/make_outputs/pallas_call | solution.py:1424

commit v2 on v1

--- a/solution.py
+++ b/solution.py
@@ -313,9 +313,8 @@
     ask[...] = jnp.broadcast_to(heads, (8, 128))
     pl.semaphore_wait(pltpu.get_barrier_semaphore(), many - 1)
     ask_pairs = [(lambda peer: ask, asks)]
-    raw_pairs = [(lambda peer: raw, every_ref)]
     spread_start(many, me, ask_pairs, send, recv, 0)
-    spread_start(many, me, raw_pairs, send, recv, 1)
+    relay_start(many, me, raw, every_ref, send, recv, 1)
     asks[me] = ask[...]
     every_ref[me] = raw[...]
     padded = sizes.padded
@@ -325,6 +324,7 @@
     first = me * depth
     block = math.gcd(many, 16)
     spread_wait(many, me, ask_pairs, send, recv, 0)
+    relay_pass(many, me, raw, every_ref, send, recv, 1)
 
     def pick(step, carry):
         found = []
@@ -349,7 +349,7 @@
     landed[me] = offer[me]
     if sizes.keep:
         prepare_tokens(sizes, table_ref, place_ref, table_t, place_t)
-    spread_wait(many, me, raw_pairs, send, recv, 1)
+    relay_wait(many, me, raw, every_ref, send, recv, 1)
 
     row_pairs = [(lambda peer: own, rows_ref)]
 

time: 156 us -> 151 us (0.968)
  Pallas kernels: 154 us -> 149 us
    pallas_call x1, Pallas kernels: 24.8 us -> 18.6 us  [remote_call(): pl.pallas_call(kernel, out_shape=out_shape, in_specs=[pl.BlockSpec(memory...]
where the time goes in v2:
time: 151 us; the launch traced here: 150 us
  Pallas kernels  149 us (99%)
    pallas_call x3, Pallas kernels, local_call(): pl.pallas_call(kernel, out_shape=out_shape, in_specs=[sm if i in smem_in...  43.9 us
    pallas_call x1, Pallas kernels, first_stage(): pl.pallas_call(functools.partial(first_kernel, sizes), out_shape=(jax.Sha...  38.6 us
    pallas_call x1, Pallas kernels, finish(): pl.pallas_call(functools.partial(finish_kernel, sizes), out_shape=tuple((...  36.3 us
    pallas_call x1, Pallas kernels, remote_call(): pl.pallas_call(kernel, out_shape=out_shape, in_specs=[pl.BlockSpec(memory...  18.6 us
    pallas_call x1, Pallas kernels, make_outputs(): pl.pallas_call(functools.partial(outputs_kernel, anchors[0].shape[0], gro...  12 us

profile of v2, /device:TPU:0, one launch (start us, length us, event | category | flops | bytes accessed | tf_op | source)
XLA Modules:
  0.0 150.4 jit_solution(14936145259214626027)
XLA Ops:
  0.7 38.6 %first_stage.1 = (s16[16,80,128]{2,1,0:T(8,128)(2,1)}, bf16[16,48,128]{2,1,0:T(8,128)(2,1)}, f32[18,136,512]{2,1,0:T(8,128)}, s32[18,8,512]{2,1,0:T(8,128)}, f32[8,128]{1,0:T(8,128)}) custom-call(s32[16,64]{1,0:T(8,128)} %question_ref.1, s32[32,256]{1,0:T(8,128)} %passage_ref.1, s32[16]{0:T(128)} %length_q.1, s32[32]{0:T(128)} %length_p.1, s32[16]{0:T(128)} %key_q.1, ...), custom_call_target="tpu_custom_call" | custom-call | tf_op jit(solution)/shard_map/first_stage/pallas_call | solution.py:396
  39.3 9.0 %tokens_forward.1 = (bf16[16,48,128]{2,1,0:T(8,128)(2,1)}, f32[16,2,128]{2,1,0:T(2,128)}, bf16[16,48,128]{2,1,0:T(8,128)(2,1)}, s32[1]{0:T(128)}) custom-call(s16[16,80,128]{2,1,0:T(8,128)(2,1)} %get-tuple-element.87.raw_ref.refs_4_, bf16[16,48,128]{2,1,0:T(8,128)(2,1)} %get-tuple-element.86.rows_ref.refs_3_, f32[18,136,512]{2,1,0:T(8,128)} %get-tuple-element.88.kept_hbm, ...), custom_call_target="tpu_custom_call" | custom-call | tf_op jit(solution)/shard_map/tokens_forward/pallas_call | solution.py:785
  48.3 18.6 %exchange_mixed.1 = (bf16[16,48,128]{2,1,0:T(8,128)(2,1)}, f32[16,2,128]{2,1,0:T(2,128)}) custom-call(bf16[16,48,128]{2,1,0:T(8,128)(2,1)} %get-tuple-element.91.part_ref, f32[16,2,128]{2,1,0:T(2,128)} %get-tuple-element.92.lse_ref), custom_call_target="tpu_custom_call" | custom-call | tf_op jit(solution)/shard_map/exchange_mixed/pallas_call | solution.py:860
  66.9 8.2 %class_stage.1 = (bf16[16,48,128]{2,1,0:T(8,128)(2,1)}, f32[256,128]{1,0:T(8,128)}, f32[512,128]{1,0:T(8,128)}, f32[2,128,128]{2,1,0:T(8,128)}, f32[2,2,128,512]...) custom-call(bf16[16,48,128]{2,1,0:T(8,128)(2,1)} %get-tuple-element.86.rows_ref.refs_3_, ...), custom_call_target="tpu_custom_call" | custom-call | tf_op jit(solution)/shard_map/class_stage/pallas_call | solution.py:785
  75.2 26.7 %tokens_backward.1 = (bf16[16,48,128]{2,1,0:T(8,128)(2,1)}, f32[2048,128]{1,0:T(8,128)}, bf16[2,4,128,128]{3,2,1,0:T(8,128)(2,1)}) custom-call(s32[1]{0:T(128)} %get-tuple-element.96.levels_ref, s16[16,80,128]{2,1,0:T(8,128)(2,1)} %get-tuple-element.87.raw_ref.refs_4_, bf16[16,48,128]{2,1,0:T(8,128)(2,1)} %get-tuple-element.97.query_ref, ...), custom_call_target="tpu_custom_call" | custom-call | tf_op jit(solution)/shard_map/tokens_backward/pallas_call | solution.py:785
  101.9 36.3 %finish.1 = (f32[8,128]{1,0:T(8,128)}, f32[1920,128]{1,0:T(8,128)}, f32[2,256,128]{2,1,0:T(8,128)}, f32[2,128,512]{2,1,0:T(8,128)}, f32[16,2,128]{2,1,0:T(2,128)...) custom-call(bf16[16,48,128]{2,1,0:T(8,128)(2,1)} %get-tuple-element., ...), custom_call_target="tpu_custom_call" | custom-call | tf_op jit(solution)/shard_map/finish/pallas_call | solution.py:1302
  138.2 12.0 %make_outputs.1 = (f32[1,1920,128]{2,1,0:T(8,128)}, f32[1,1920,128]{2,1,0:T(8,128)}, f32[1920,128]{1,0:T(8,128)}, f32[1920,128]{1,0:T(8,128)}, f32[1,1920,128]{2...) custom-call(f32[8,128]{1,0:T(8,128)} %get-tuple-element.108.refs_0_,, ...), custom_call_target="tpu_custom_call" | custom-call | tf_op jit(solution)/shard_map/make_outputs/pallas_call | solution.py:1424

commit v3 on v2

--- a/solution.py
+++ b/solution.py
@@ -262,7 +262,7 @@
     key_q,
     valid_q,
     key_p,
-    table_ref,
+    table_hbm,
     place_ref,
     every_ref,
     rows_ref,
@@ -279,6 +279,8 @@
     own,
     table_t,
     place_t,
+    table_ref,
+    fetch,
     send,
     recv,
 ):
@@ -287,6 +289,8 @@
     each = count_q + count_p
     depth = sizes.depth
     half = count_q // 2
+    load = pltpu.make_async_copy(table_hbm, table_ref, fetch.at[0])
+    load.start()
     me = greet_all(many)
     lane = iota((1, 128), 1)
     for seq in range(count_p):
@@ -320,6 +324,7 @@
     padded = sizes.padded
     if padded > depth:
         low_ref[...] = jnp.zeros_like(low_ref)
+    load.wait()
     low_ref[0:depth, :] = low16(table_ref[...])
     first = me * depth
     block = math.gcd(many, 16)
@@ -402,7 +407,7 @@
             jax.ShapeDtypeStruct((kept, 8, SPAN), jnp.int32),
             jax.ShapeDtypeStruct((8, 128), jnp.float32),
         ),
-        in_specs=[vm, vm, sm, sm, sm, sm, sm, vm, vm],
+        in_specs=[vm, vm, sm, sm, sm, sm, sm, pl.BlockSpec(memory_space=pl.ANY), vm],
         out_specs=[vm] * 5,
         scratch_shapes=[
             pltpu.VMEM((RAW_ROWS, 128), jnp.int32),
@@ -415,6 +420,8 @@
             pltpu.VMEM((both, 128), jnp.bfloat16),
             pltpu.VMEM((128, padded), jnp.bfloat16),
             pltpu.VMEM((2, 2, 128, CHUNK), jnp.bfloat16),
+            pltpu.VMEM((sizes.depth, 128), jnp.float32),
+            pltpu.SemaphoreType.DMA((1,)),
             pltpu.SemaphoreType.DMA((4, many)),
             pltpu.SemaphoreType.DMA((4, many)),
         ],
@@ -589,7 +596,7 @@
     kept_hbm,
     entry_hbm,
     count_ref,
-    table_ref,
+    table_hbm,
     place_ref,
     attn_ref,
     vec_ref,
@@ -611,6 +618,8 @@
     kept_ref,
     entry_ref,
     load,
+    table_ref,
+    fetch,
 ):
     loads = load_kept(sizes, kept_hbm, entry_hbm, kept_ref, entry_ref, load)
     first = lax.axis_index("dp") * sizes.depth
@@ -715,6 +724,9 @@
 
     @pl.when(start > begin)
     def _():
+        copy = pltpu.make_async_copy(table_hbm, table_ref, fetch.at[0])
+        copy.start()
+        copy.wait()
         prepare_tokens(sizes, table_ref, place_ref, table_t, place_t)
 
         def one_level(state):
@@ -766,6 +778,8 @@
         pltpu.VMEM((kept, 136, SPAN), jnp.float32),
         pltpu.VMEM((kept, 8, SPAN), jnp.int32),
         pltpu.SemaphoreType.DMA((2, 2)),
+        pltpu.VMEM((sizes.depth, 128), jnp.float32),
+        pltpu.SemaphoreType.DMA((1,)),
     ]
 
 
@@ -815,7 +829,7 @@
         + kept_scratch(sizes),
         "tokens_forward",
         smem_out=(3,),
-        any_in=(2, 3),
+        any_in=(2, 3, 5),
     )
 
 
@@ -904,7 +918,7 @@
     grad_ref,
     kept_hbm,
     entry_hbm,
-    table_ref,
+    table_hbm,
     place_ref,
     attn_ref,
     vec_ref,
@@ -925,6 +939,8 @@
     kept_ref,
     entry_ref,
     load,
+    table_ref,
+    fetch,
 ):
     loads = load_kept(sizes, kept_hbm, entry_hbm, kept_ref, entry_ref, load)
     first = lax.axis_index("dp") * sizes.depth
@@ -935,6 +951,9 @@
 
     @pl.when(again)
     def _():
+        copy = pltpu.make_async_copy(table_hbm, table_ref, fetch.at[0])
+        copy.start()
+        copy.wait()
         prepare_tokens(sizes, table_ref, place_ref, table_t, place_t)
 
     for ref in (d_table_ref, d_place_ref, d_attn_ref, d_query_q, d_query_p, acc_gain, acc_shift, acc_value):
@@ -1092,7 +1111,7 @@
         + kept_scratch(sizes),
         "tokens_backward",
         smem_in=(0,),
-        any_in=(6, 7),
+        any_in=(6, 7, 8),
     )
 
 
@@ -1119,7 +1138,7 @@
     many = sizes.many
     count_q, count_p = sizes.count
     depth = sizes.depth
-    (query_ref, slice_ref, d_table_ref, rows_ref, raw_ref, xa_q, xa_p, d_out, d_ffn, d_mid) = refs[:10]
+    (query_ref, slice_ref, d_table_hbm, rows_ref, raw_ref, xa_q, xa_p, d_out, d_ffn_hbm, d_mid) = refs[:10]
     place_ref, attn_ref, vec_ref = refs[10:13]
     state = refs[13:33]
     norm_ref, g_word, g_place, g_attn, g_vec = refs[33:38]
@@ -1128,9 +1147,13 @@
     mine = refs[63:68]
     theirs = refs[68:73]
     (query_all, slice_all, scalar_all, land_query, land_slice, own_query, own_slice, tile, table_t) = refs[73:82]
-    half_query, far_query, half_slice, far_slice = refs[82:86]
-    send, recv, load, pair_send, pair_recv = refs[86:91]
-    loads = []
+    half_query, far_query, half_slice, far_slice, d_table_ref, d_ffn = refs[82:88]
+    send, recv, load, pair_send, pair_recv = refs[88:93]
+    loads, early = ([], [])
+    for index, (source, target) in enumerate(((d_table_hbm, d_table_ref), (d_ffn_hbm, d_ffn))):
+        copy = pltpu.make_async_copy(source, target, load.at[20 + index])
+        copy.start()
+        early.append(copy)
     for index in range(20):
         copy = pltpu.make_async_copy(state[index], held[index], load.at[index])
         copy.start()
@@ -1163,6 +1186,8 @@
 
     g_vec[...] = d_mid[...]
     tops = []
+    for copy in early:
+        copy.wait()
     first = me * depth
     table_t[...] = jnp.zeros_like(table_t)
     rest = jnp.zeros((1, 1), jnp.float32)
@@ -1305,7 +1330,7 @@
             jax.ShapeDtypeStruct(shape, f32)
             for shape in [(8, 128), shapes[0], shapes[1], shapes[2], (16, 2, 128)] + shapes
         ),
-        in_specs=[vm] * len(inputs) + [hbm] * 20,
+        in_specs=[hbm if i in (2, 8) else vm for i in range(len(inputs))] + [hbm] * 20,
         out_specs=[vm] * 10,
         scratch_shapes=[pltpu.VMEM(value.shape, f32) for value in flat]
         + [pltpu.VMEM(shape, jnp.bfloat16 if kind < 4 else f32) for kind, shape in enumerate(shapes)] * 2
@@ -1323,9 +1348,11 @@
             pltpu.VMEM((many // NEAR, both, 128), jnp.bfloat16),
             pltpu.VMEM((many // NEAR, sizes.lines, 128), sizes.kind),
             pltpu.VMEM((many // NEAR, sizes.lines, 128), sizes.kind),
+            pltpu.VMEM(d_table.shape, f32),
+            pltpu.VMEM(d_ffn.shape, f32),
             pltpu.SemaphoreType.DMA((8, many)),
             pltpu.SemaphoreType.DMA((8, many)),
-            pltpu.SemaphoreType.DMA((20,)),
+            pltpu.SemaphoreType.DMA((22,)),
             pltpu.SemaphoreType.DMA((5,)),
             pltpu.SemaphoreType.DMA((5,)),
         ],

time: 151 us -> 149 us (0.987)
  no operation moved by 1% of the time
where the time goes in v3:
time: 149 us
  Pallas kernels  148 us (99%)
    pallas_call x3, Pallas kernels, local_call(): pl.pallas_call(kernel, out_shape=out_shape, in_specs=[sm if i in smem_in...  43.4 us
    pallas_call x1, Pallas kernels, first_stage(): pl.pallas_call(functools.partial(first_kernel, sizes), out_shape=(jax.Sha...  38.3 us
    pallas_call x1, Pallas kernels, finish(): pl.pallas_call(functools.partial(finish_kernel, sizes), out_shape=tuple((...  35.7 us
    pallas_call x1, Pallas kernels, remote_call(): pl.pallas_call(kernel, out_shape=out_shape, in_specs=[pl.BlockSpec(memory...  18.6 us
    pallas_call x1, Pallas kernels, make_outputs(): pl.pallas_call(functools.partial(outputs_kernel, anchors[0].shape[0], gro...  12 us

profile of v3, /device:TPU:0, one launch (start us, length us, event | category | flops | bytes accessed | tf_op | source)
XLA Modules:
  0.0 148.9 jit_solution(14329544730290556307)
XLA Ops:
  0.7 38.3 %first_stage.1 = (s16[16,80,128]{2,1,0:T(8,128)(2,1)}, bf16[16,48,128]{2,1,0:T(8,128)(2,1)}, f32[18,136,512]{2,1,0:T(8,128)}, s32[18,8,512]{2,1,0:T(8,128)}, f32[8,128]{1,0:T(8,128)}) custom-call(s32[16,64]{1,0:T(8,128)} %question_ref.1, s32[32,256]{1,0:T(8,128)} %passage_ref.1, s32[16]{0:T(128)} %length_q.1, s32[32]{0:T(128)} %length_p.1, s32[16]{0:T(128)} %key_q.1, ...), custom_call_target="tpu_custom_call" | custom-call | tf_op jit(solution)/shard_map/first_stage/pallas_call | solution.py:401
  39.0 8.7 %tokens_forward.1 = (bf16[16,48,128]{2,1,0:T(8,128)(2,1)}, f32[16,2,128]{2,1,0:T(2,128)}, bf16[16,48,128]{2,1,0:T(8,128)(2,1)}, s32[1]{0:T(128)}) custom-call(s16[16,80,128]{2,1,0:T(8,128)(2,1)} %get-tuple-element.87.raw_ref.refs_4_, bf16[16,48,128]{2,1,0:T(8,128)(2,1)} %get-tuple-element.86.rows_ref.refs_3_, f32[18,136,512]{2,1,0:T(8,128)} %get-tuple-element.88.kept_hbm, ...), custom_call_target="tpu_custom_call" | custom-call | tf_op jit(solution)/shard_map/tokens_forward/pallas_call | solution.py:799
  47.7 18.6 %exchange_mixed.1 = (bf16[16,48,128]{2,1,0:T(8,128)(2,1)}, f32[16,2,128]{2,1,0:T(2,128)}) custom-call(bf16[16,48,128]{2,1,0:T(8,128)(2,1)} %get-tuple-element.91.part_ref, f32[16,2,128]{2,1,0:T(2,128)} %get-tuple-element.92.lse_ref), custom_call_target="tpu_custom_call" | custom-call | tf_op jit(solution)/shard_map/exchange_mixed/pallas_call | solution.py:874
  66.4 8.2 %class_stage.1 = (bf16[16,48,128]{2,1,0:T(8,128)(2,1)}, f32[256,128]{1,0:T(8,128)}, f32[512,128]{1,0:T(8,128)}, f32[2,128,128]{2,1,0:T(8,128)}, f32[2,2,128,512]...) custom-call(bf16[16,48,128]{2,1,0:T(8,128)(2,1)} %get-tuple-element.86.rows_ref.refs_3_, ...), custom_call_target="tpu_custom_call" | custom-call | tf_op jit(solution)/shard_map/class_stage/pallas_call | solution.py:799
  74.6 26.4 %tokens_backward.1 = (bf16[16,48,128]{2,1,0:T(8,128)(2,1)}, f32[2048,128]{1,0:T(8,128)}, bf16[2,4,128,128]{3,2,1,0:T(8,128)(2,1)}) custom-call(s32[1]{0:T(128)} %get-tuple-element.96.levels_ref, s16[16,80,128]{2,1,0:T(8,128)(2,1)} %get-tuple-element.87.raw_ref.refs_4_, bf16[16,48,128]{2,1,0:T(8,128)(2,1)} %get-tuple-element.97.query_ref, ...), custom_call_target="tpu_custom_call" | custom-call | tf_op jit(solution)/shard_map/tokens_backward/pallas_call | solution.py:799
  101.1 35.7 %finish.1 = (f32[8,128]{1,0:T(8,128)}, f32[1920,128]{1,0:T(8,128)}, f32[2,256,128]{2,1,0:T(8,128)}, f32[2,128,512]{2,1,0:T(8,128)}, f32[16,2,128]{2,1,0:T(2,128)...) custom-call(bf16[16,48,128]{2,1,0:T(8,128)(2,1)} %get-tuple-element., ...), custom_call_target="tpu_custom_call" | custom-call | tf_op jit(solution)/shard_map/finish/pallas_call | solution.py:1327
  136.7 12.0 %make_outputs.1 = (f32[1,1920,128]{2,1,0:T(8,128)}, f32[1,1920,128]{2,1,0:T(8,128)}, f32[1920,128]{1,0:T(8,128)}, f32[1920,128]{1,0:T(8,128)}, f32[1,1920,128]{2...) custom-call(f32[8,128]{1,0:T(8,128)} %get-tuple-element.108.refs_0_,, ...), custom_call_target="tpu_custom_call" | custom-call | tf_op jit(solution)/shard_map/make_outputs/pallas_call | solution.py:1451
